TPU v7x, 256 devices: a whole 4x4x8 slice. The times are simulated.
256 devices in a mesh: table: 16 (over z, core), row: 16 (over y, x).
Axes of the slice: x: 4, y: 4, z: 8, core: 2. Of those that a mesh axis runs over, the one named last changes fastest.
Arguments:
- dense_feat: bfloat16 [65536, 128], P(('table', 'row')), may hold values from -6 to 6
- pooled: bfloat16 [65536, 2048], P(('table', 'row')), may hold values from -6 to 6
- labels: int32 [65536], P(('table', 'row')), may hold values 0 or 1
- cross_down: bfloat16 [2176, 256], replicated, may hold values from -0.125 to 0.125
- cross_up: bfloat16 [256, 2176], replicated, may hold values from -0.375 to 0.375
- cross_bias: float32 [2176], replicated, may hold values from -3 to 3
- w_hidden1: bfloat16 [2176, 1024], replicated, may hold values from -0.125 to 0.125
- bias1: float32 [1024], replicated, may hold values from -3 to 3
- w_hidden2: bfloat16 [1024, 1024], replicated, may hold values from -0.1875 to 0.1875
- bias2: float32 [1024], replicated, may hold values from -3 to 3
- w_logit: float32 [1024], replicated, may hold values from -0.6 to 0.6
- lookup_slots: int32 [16, 65536, 4], P('table'), may hold values from 0 to 16383, as said below
Outputs:
- row_grads: float32 [16, 16384, 128], P('table', 'row')
- grad_cross_down: float32 [2176, 256], P('row')
- grad_cross_up: float32 [256, 2176], P('row')
- grad_cross_bias: float32 [2176], P('row')
- grad_hidden1: float32 [2176, 1024], P('row')
- grad_bias1: float32 [1024], P('row')
- grad_hidden2: float32 [1024, 1024], P('row')
- grad_bias2: float32 [1024], P('row')
- grad_logit: float32 [1024], P('row')
Inputs may be any that keep to these rules, and one draw needn't show every extreme that they name: `lookup_slots`: row shard r of a table owns the slots r * 1024 to (r + 1) * 1024 - 1; a lookup's slot is the deduplicated row that it reads.
All inputs are finite; a program needn't handle non-finite values. No bound on the sum of `labels` on one device may be relied on, other than what follows from the above.
Results may differ from a plain program's by a relative error of at most 0.015.
Values may be sent and summed in bfloat16 or wider, within the bound.
A program may use at most 128 MiB of HBM per device.

v0:
```python
import jax
import jax.numpy as jnp
from jax import lax
from jax.sharding import PartitionSpec as P

loss_scale = 16.0


def swish_slope(value):
    sig = jax.nn.sigmoid(value)
    return sig * (1.0 + value * (1.0 - sig))


def dense_backward(
    dense_feat,
    pooled,
    labels,
    cross_down,
    cross_up,
    cross_bias,
    w_hidden1,
    bias1,
    w_hidden2,
    bias2,
    w_logit,
):
    stacked = jnp.concatenate([dense_feat, pooled], axis=1)
    stacked_wide = stacked.astype(jnp.float32)
    reduced = jnp.dot(stacked, cross_down, preferred_element_type=jnp.float32).astype(jnp.bfloat16)
    widened = jnp.dot(reduced, cross_up, preferred_element_type=jnp.float32) + cross_bias
    crossed = (stacked_wide * widened + stacked_wide).astype(jnp.bfloat16)
    pre_first = jnp.dot(crossed, w_hidden1, preferred_element_type=jnp.float32) + bias1
    act_first = jax.nn.silu(pre_first).astype(jnp.bfloat16)
    pre_second = jnp.dot(act_first, w_hidden2, preferred_element_type=jnp.float32) + bias2
    act_second = jax.nn.silu(pre_second).astype(jnp.bfloat16)
    act_wide = act_second.astype(jnp.float32)
    logits = jnp.sum(act_wide * w_logit, axis=1)
    delta_logit = loss_scale * (jax.nn.sigmoid(logits) - labels.astype(jnp.float32))
    delta_second = (delta_logit[:, None] * w_logit[None, :] * swish_slope(pre_second)).astype(
        jnp.bfloat16
    )
    grad_logit = jnp.sum(act_wide * delta_logit[:, None], axis=0)
    grad_hidden2 = jnp.dot(act_first.T, delta_second, preferred_element_type=jnp.float32)
    grad_bias2 = jnp.sum(delta_second.astype(jnp.float32), axis=0)
    back_first = jnp.dot(delta_second, w_hidden2.T, preferred_element_type=jnp.float32)
    delta_first = (back_first * swish_slope(pre_first)).astype(jnp.bfloat16)
    grad_hidden1 = jnp.dot(crossed.T, delta_first, preferred_element_type=jnp.float32)
    grad_bias1 = jnp.sum(delta_first.astype(jnp.float32), axis=0)
    delta_crossed = jnp.dot(delta_first, w_hidden1.T, preferred_element_type=jnp.float32)
    delta_widened = (delta_crossed * stacked_wide).astype(jnp.bfloat16)
    grad_cross_up = jnp.dot(reduced.T, delta_widened, preferred_element_type=jnp.float32)
    grad_cross_bias = jnp.sum(delta_widened.astype(jnp.float32), axis=0)
    delta_reduced = jnp.dot(delta_widened, cross_up.T, preferred_element_type=jnp.float32).astype(
        jnp.bfloat16
    )
    grad_cross_down = jnp.dot(stacked.T, delta_reduced, preferred_element_type=jnp.float32)
    delta_stacked = delta_crossed * (widened + 1.0) + jnp.dot(
        delta_reduced, cross_down.T, preferred_element_type=jnp.float32
    )
    grads = (
        grad_cross_down,
        grad_cross_up,
        grad_cross_bias,
        grad_hidden1,
        grad_bias1,
        grad_hidden2,
        grad_bias2,
        grad_logit,
    )
    return (grads, delta_stacked)


def local(
    dense_feat,
    pooled,
    labels,
    cross_down,
    cross_up,
    cross_bias,
    w_hidden1,
    bias1,
    w_hidden2,
    bias2,
    w_logit,
    lookup_slots,
):
    grads, delta_stacked = dense_backward(
        dense_feat,
        pooled,
        labels,
        cross_down,
        cross_up,
        cross_bias,
        w_hidden1,
        bias1,
        w_hidden2,
        bias2,
        w_logit,
    )
    width = dense_feat.shape[1]
    batch_dev = dense_feat.shape[0]
    n_table = lax.axis_size("table")
    n_row = lax.axis_size("row")
    tab_grp = lookup_slots.shape[0]
    hot_count = lookup_slots.shape[2]
    tables = tab_grp * n_table
    u_shard = batch_dev * n_table * hot_count // 16
    pooled_grad = delta_stacked[:, width:].astype(jnp.bfloat16).reshape(batch_dev, tables, width)
    received = lax.all_to_all(pooled_grad, "table", split_axis=1, concat_axis=0, tiled=True)
    row_pos = lax.axis_index("row")
    arranged = lookup_slots.reshape(tab_grp, n_table, n_row, batch_dev, hot_count)
    ordered = jnp.transpose(arranged, (0, 2, 1, 3, 4)).reshape(
        tab_grp, n_row * n_table * batch_dev, hot_count
    )
    in_shard = ordered - row_pos * u_shard
    in_shard = jnp.where((in_shard >= 0) & (in_shard < u_shard), in_shard, u_shard)
    initial = jnp.zeros((tab_grp, u_shard, width), jnp.float32)
    values = lax.all_gather(received, "row", axis=0, tiled=True)[:, 0].astype(jnp.float32)
    current = initial[0]
    for which in range(hot_count):
        current = current + jax.ops.segment_sum(values, in_shard[0, :, which], num_segments=u_shard)
    parts = [current]
    row_grads = jnp.stack(parts)
    g_down, g_up, g_cbias, g_first, g_bfirst, g_second, g_bsecond, g_logit = grads
    parted = (
        lax.psum_scatter(g_down, "row", scatter_dimension=0, tiled=True),
        lax.psum_scatter(g_up, "row", scatter_dimension=0, tiled=True),
        lax.psum_scatter(g_cbias, "row", scatter_dimension=0, tiled=True),
        lax.psum_scatter(g_first, "row", scatter_dimension=0, tiled=True),
        lax.psum_scatter(g_bfirst, "row", scatter_dimension=0, tiled=True),
        lax.psum_scatter(g_second, "row", scatter_dimension=0, tiled=True),
        lax.psum_scatter(g_bsecond, "row", scatter_dimension=0, tiled=True),
        lax.psum_scatter(g_logit, "row", scatter_dimension=0, tiled=True),
    )
    s_down, s_up, s_cbias, s_first, s_bfirst, s_second, s_bsecond, s_logit = parted
    totals = lax.psum(
        (s_down, s_up, s_cbias, s_first, s_bfirst, s_second, s_bsecond, s_logit), "table"
    )
    return (
        row_grads,
        totals[0],
        totals[1],
        totals[2],
        totals[3],
        totals[4],
        totals[5],
        totals[6],
        totals[7],
    )


def solution(mesh):
    in_specs = (
        P(("table", "row"), None),
        P(("table", "row"), None),
        P(("table", "row")),
        P(),
        P(),
        P(),
        P(),
        P(),
        P(),
        P(),
        P(),
        P("table", None, None),
    )
    out_specs = (
        P("table", "row", None),
        P("row", None),
        P("row", None),
        P("row"),
        P("row", None),
        P("row"),
        P("row", None),
        P("row"),
        P("row"),
    )
    return jax.shard_map(local, mesh=mesh, in_specs=in_specs, out_specs=out_specs, check_vma=False)
```

profile of v0, /device:TPU:2, one launch (start us, length us, event | category | flops | bytes accessed | tf_op | source)
XLA Modules:
  0.0 1920.4 jit_solution(16378032982188633010)
XLA Ops:
  16.2 2.8 convert_reduce_fusion
  19.0 1.9 fusion.31
  20.9 1.8 convolution_convert_fusion
  22.7 1.9 fusion.30
  24.7 2.8 fusion.26
  28.5 6.4 fusion.23
  37.8 1.9 copy_bitcast_fusion
  39.7 35.9 %all_to_all.18 = bf16[256,16,128]{2,0,1:T(8,128)(2,1)} all-to-all(bf16[256,16,128]{2,0,1:T(8,128)(2,1)S(1)} %copy_bitcast_fusion), channel_id=1, replica_groups=mesh['table'=16,'row'=16] {'table'}, dimensions={1} | all-to-all | bytes 2097152 | tf_op jit(solution)/shard_map/all_to_all | solution.py:109
  79.1 45.5 %all-reduce.13.cloned.1.call-done = f32[256,2176]{1,0:T(8,128)} async-done(((f32[256,2176]{1,0:T(8,128)}), f32[256,2176]{1,0:T(8,128)}) %all-reduce.13.cloned.1.call-update) | async-done | bytes 2228240
  124.6 1.6 constant_dynamic-slice_fusion
  126.2 81.3 %reduce-scatter.10.cloned.1.call-done = f32[136,256]{1,0:T(8,128)} async-done(((f32[2176,256]{1,0:T(8,128)}), f32[136,256]{1,0:T(8,128)}) %reduce-scatter.10.cloned.1.call-update) | async-done | bytes 139280
  207.5 85.7 %reduce-scatter.8.cloned.1.call-done = f32[64,1024]{1,0:T(8,128)} async-done(((f32[1024,1024]{1,0:T(8,128)}), f32[64,1024]{1,0:T(8,128)}) %reduce-scatter.8.cloned.1.call-update) | async-done | bytes 262160 | tf_op jit(solution)/shard_map/reduce_scatter | solution.py:131
  293.2 94.8 %reduce-scatter.12.cloned.1.call-done = f32[136,1024]{1,0:T(8,128)} async-done(((f32[2176,1024]{1,0:T(8,128)}), f32[136,1024]{1,0:T(8,128)}) %reduce-scatter.12.cloned.1.call-update) | async-done | bytes 557072
  389.5 68.0 %all-reduce.7 = (f32[2176]{0:T(1024)S(1)}, f32[1024]{0:T(1024)S(1)}, f32[1024]{0:T(1024)S(1)}, f32[1024]{0:T(1024)S(1)}) all-reduce(f32[2176]{0:T(1024)S(1)} %get-tuple-element.23, f32[1024]{0:T(1024)S(1)} %get-tuple-element.34, f32[1024]{0:T(1024)S(1)} %get-tuple-element.21, ...), channel_id=4, replica_groups=mesh['table'=16,'row'=16] {'row'}, use_global_device_ids=true, to_apply=%region_10.11.clone | all-reduce | flops 5248 | bytes 41984
  458.5 25.7 %all-reduce.8 = (f32[136]{0:T(256)}, f32[64]{0:T(128)}, f32[64]{0:T(128)}, f32[64]{0:T(128)}) all-reduce(f32[136]{0:T(256)S(1)} %dynamic-slice.5, f32[64]{0:T(128)S(1)} %dynamic-slice.9, f32[64]{0:T(128)S(1)} %dynamic-slice.11, f32[64]{0:T(128)S(1)} %dynamic-slice.13), channel_id=1, replica_groups=mesh['table'=16,'row'=16] {'table'}, use_global_device_ids=true, to_apply=%region_11.12 | all-reduce | flops 328 | bytes 2624 | tf_op jit(solution)/shard_map/psum | solution.py:136
  484.1 22.1 %all-gather.2.cloned.1.call-done = bf16[65536,1,128]{2,0,1:T(8,128)(2,1)} async-done(((bf16[4096,1,128]{2,0,1:T(8,128)(2,1)}), bf16[65536,1,128]{2,0,1:T(8,128)(2,1)}) %all-gather.2.cloned.1.call-update) | async-done | bytes 16777232 | tf_op jit(solution)/shard_map/all_gather | solution.py:118
  506.3 349.8 %scatter_custom_fusion.1 = f32[1024,128]{1,0:T(8,128)S(1)} fusion(s32[65536]{0:T(1024)S(1)} %bitcast.75, bf16[65536,1,128]{2,0,1:T(8,128)(2,1)} %all-gather.2.cloned.1.call-done, f32[]{:T(128)} %constant.6.clone.1), kind=kCustom, calls=%fused_computation.8 | custom fusion | flops 16777216 | bytes 17301508 | tf_op jit(solution)/shard_map/scatter-add | solution.py:121
  856.1 349.9 %scatter_custom_fusion = f32[1024,128]{1,0:T(8,128)S(1)} fusion(s32[65536]{0:T(1024)S(1)} %bitcast.74, bf16[65536,1,128]{2,0,1:T(8,128)(2,1)} %all-gather.2.cloned.1.call-done, f32[]{:T(128)} %constant.6.clone.1), kind=kCustom, calls=%fused_computation.10 | custom fusion | flops 16777216 | bytes 17301508 | tf_op jit(solution)/shard_map/scatter-add | solution.py:121
  1206.1 349.9 %scatter_custom_fusion.3 = f32[1024,128]{1,0:T(8,128)S(1)} fusion(s32[65536]{0:T(1024)S(1)} %bitcast.73, bf16[65536,1,128]{2,0,1:T(8,128)(2,1)} %all-gather.2.cloned.1.call-done, f32[]{:T(128)} %constant.6.clone.1), kind=kCustom, calls=%fused_computation.4 | custom fusion | flops 16777216 | bytes 17301508 | tf_op jit(solution)/shard_map/scatter-add | solution.py:121
  1555.9 350.1 %scatter_custom_fusion.2 = f32[1024,128]{1,0:T(8,128)S(1)} fusion(f32[1024,128]{1,0:T(8,128)S(1)} %add.117, s32[65536]{0:T(1024)S(1)} %bitcast.72, bf16[65536,1,128]{2,0,1:T(8,128)(2,1)} %all-gather.2.cloned.1.call-done), kind=kCustom, calls=%fused_computation.6 | custom fusion | flops 16777216 | bytes 17301504 | tf_op jit(solution)/shard_map/scatter-add | solution.py:121
  1906.9 1.6 copy.38
  1908.4 1.6 copy.39
  1910.0 1.9 copy.40
  1911.9 1.7 copy.41
  (78 shorter events, 17.5 us)
Async XLA Ops:
  7.2 6.3 copy-start
  7.2 117.4 %all-reduce.13.cloned.1.call-start = ((), (), s32[]{:S(2)}) async-start(), calls=%async_computation.6 | async-start | bytes 4456448
  7.2 2.4 copy-start.6
  8.3 1.9 copy-start.5
  8.3 1.9 copy-start.13
  9.7 2.3 copy-start.4
  10.2 1.8 copy-start.16
  12.0 1.5 copy-start.2
  12.0 1.5 copy-start.14
  12.0 1.5 copy-start.17
  13.5 1.6 copy-start.19
  16.1 2.8 copy-start.8
  20.9 186.6 %reduce-scatter.10.cloned.1.call-start = ((), (), s32[]{:S(2)}) async-start(), calls=%async_computation.7 | async-start | bytes 2367488
  22.7 2.0 copy-start.12
  22.7 2.0 copy-start.20
  24.6 268.6 %reduce-scatter.8.cloned.1.call-start = ((), (), s32[]{:S(2)}) async-start(), calls=%async_computation.5 | async-start | bytes 4456448 | tf_op jit(solution)/shard_map/reduce_scatter | solution.py:131
  27.5 360.5 %reduce-scatter.12.cloned.1.call-start = ((), (), s32[]{:S(2)}) async-start(), calls=%async_computation.8 | async-start | bytes 9469952
  34.9 1.3 copy-start.7
  35.0 471.3 %all-gather.2.cloned.1.call-start = ((), (), s32[]{:S(2)}) async-start(), calls=%async_computation.4 | async-start | bytes 17825792 | tf_op jit(solution)/shard_map/all_gather | solution.py:118
  36.2 1.6 copy-start.3
  39.7 36.2 %copy-start.10 = (s32[1,65536,4]{1,2,0:T(4,128)S(1)}, s32[1,65536,4]{1,2,0:T(4,128)}, u32[]{:S(2)}) copy-start(s32[1,65536,4]{1,2,0:T(4,128)} %param.23) | copy-start | bytes 3145732
  75.6 1831.2 %all-reduce.15.cloned.1.call-start = ((), (), s32[]{:S(2)}) async-start(), calls=%async_computation.9 | async-start | bytes 2195456 | tf_op jit(solution)/shard_map/psum | solution.py:136
  76.3 1.2 copy-start.18
  1555.9 357.7 %copy-start.1 = (bf16[1024,1024]{1,0:T(8,128)(2,1)S(1)}, bf16[1024,1024]{1,0:T(8,128)(2,1)}, u32[]{:S(2)}) copy-start(bf16[1024,1024]{1,0:T(8,128)(2,1)} %param.20) | copy-start | bytes 6291460
  (3 other events, 3.1 us)
Sparse Core Ops, SparseCore 0:
  21.0 103.5 all-reduce.12
  128.2 79.2 reduce-scatter.9
  211.1 82.0 reduce-scatter.7
  297.3 90.7 reduce-scatter.11
  390.3 115.9 all-gather.1
  509.3 112.1 all-reduce.14
where the time goes:
time: 1920 us
  other arithmetic  1400 us (73%)
  waiting for transfers between devices  330 us (17%)
  blocking collectives  130 us (7%)
  matrix products  22.4 us (1%)
    scatter-add x4, other arithmetic, local(): jax.ops.segment_sum(values, in_shard[0, :, which], num_segments=u_shard)  1400 us
    unnamed x9, waiting for transfers between devices  222 us
    reduce_scatter x1, waiting for transfers between devices, local(): lax.psum_scatter(g_second, 'row', scatter_dimension=0, tiled=True)  85.7 us
    unnamed x1, blocking collectives  68 us
  transfers between devices with their start and end apart: 6, of which 5 were waited for; matrix products, arithmetic and copies ran while one was open for 74% of the time, Pallas kernels for 0%

commit v1 on v0

--- a/solution.py
+++ b/solution.py
@@ -1,6 +1,8 @@
 import jax
 import jax.numpy as jnp
 from jax import lax
+from jax.experimental import pallas as pl
+from jax.experimental.pallas import tpu as pltpu
 from jax.sharding import PartitionSpec as P
 
 loss_scale = 16.0
@@ -70,6 +72,62 @@
     return (grads, delta_stacked)
 
 
+def scatter_kernel(s_ref, v_ref, o_ref, wide, *accs):
+    count = v_ref.shape[0]
+    slots, width = o_ref.shape
+    unroll = 16
+
+    def clear(i, c):
+        for acc in accs:
+            acc[pl.ds(pl.multiple_of(i * 256, 256), 256), :] = jnp.zeros((256, width), jnp.float32)
+        return c
+
+    lax.fori_loop(0, slots // 256, clear, 0)
+    wide[...] = v_ref[...].astype(jnp.float32)
+
+    def step(g, c):
+        base = g * unroll
+        for i in range(0, unroll, 2):
+            row0 = wide[pl.ds(base + i, 1), :]
+            row1 = wide[pl.ds(base + i + 1, 1), :]
+            for which, acc in enumerate(accs):
+                s0 = s_ref[which * count + base + i]
+                s1 = s_ref[which * count + base + i + 1]
+                old0 = acc[pl.ds(s0, 1), :]
+                old1 = acc[pl.ds(s1, 1), :]
+                new0 = old0 + row0
+                new1 = jnp.where(s0 == s1, new0, old1) + row1
+                acc[pl.ds(s0, 1), :] = new0
+                acc[pl.ds(s1, 1), :] = new1
+        return c
+
+    lax.fori_loop(0, count // unroll, step, 0)
+
+    def finish(i, c):
+        at = pl.ds(pl.multiple_of(i * 128, 128), 128)
+        total = accs[0][at, :]
+        for acc in accs[1:]:
+            total = total + acc[at, :]
+        o_ref[at, :] = total.astype(o_ref.dtype)
+        return c
+
+    lax.fori_loop(0, slots // 128, finish, 0)
+
+
+def scatter_rows(slots, values):
+    count, width = values.shape
+    total_slots = slots.size
+    return pl.pallas_call(
+        scatter_kernel,
+        out_shape=jax.ShapeDtypeStruct((total_slots, width), jnp.bfloat16),
+        in_specs=[pl.BlockSpec(memory_space=pltpu.SMEM), pl.BlockSpec(memory_space=pltpu.VMEM)],
+        out_specs=pl.BlockSpec(memory_space=pltpu.VMEM),
+        scratch_shapes=[pltpu.VMEM((count, width), jnp.float32)]
+        + [pltpu.VMEM((total_slots, width), jnp.float32)] * (slots.size // count),
+        compiler_params=pltpu.CompilerParams(vmem_limit_bytes=58 << 20),
+    )(slots, values)
+
+
 def local(
     dense_feat,
     pooled,
@@ -97,56 +155,32 @@
         bias2,
         w_logit,
     )
+    batch_dev = dense_feat.shape[0]
     width = dense_feat.shape[1]
-    batch_dev = dense_feat.shape[0]
     n_table = lax.axis_size("table")
     n_row = lax.axis_size("row")
-    tab_grp = lookup_slots.shape[0]
     hot_count = lookup_slots.shape[2]
-    tables = tab_grp * n_table
-    u_shard = batch_dev * n_table * hot_count // 16
-    pooled_grad = delta_stacked[:, width:].astype(jnp.bfloat16).reshape(batch_dev, tables, width)
+    samples = n_table * batch_dev
+    row_pos = lax.axis_index("row")
+    pooled_grad = delta_stacked[:, width:].astype(jnp.bfloat16).reshape(batch_dev, n_table, width)
     received = lax.all_to_all(pooled_grad, "table", split_axis=1, concat_axis=0, tiled=True)
-    row_pos = lax.axis_index("row")
-    arranged = lookup_slots.reshape(tab_grp, n_table, n_row, batch_dev, hot_count)
-    ordered = jnp.transpose(arranged, (0, 2, 1, 3, 4)).reshape(
-        tab_grp, n_row * n_table * batch_dev, hot_count
-    )
-    in_shard = ordered - row_pos * u_shard
-    in_shard = jnp.where((in_shard >= 0) & (in_shard < u_shard), in_shard, u_shard)
-    initial = jnp.zeros((tab_grp, u_shard, width), jnp.float32)
-    values = lax.all_gather(received, "row", axis=0, tiled=True)[:, 0].astype(jnp.float32)
-    current = initial[0]
-    for which in range(hot_count):
-        current = current + jax.ops.segment_sum(values, in_shard[0, :, which], num_segments=u_shard)
-    parts = [current]
-    row_grads = jnp.stack(parts)
-    g_down, g_up, g_cbias, g_first, g_bfirst, g_second, g_bsecond, g_logit = grads
-    parted = (
-        lax.psum_scatter(g_down, "row", scatter_dimension=0, tiled=True),
-        lax.psum_scatter(g_up, "row", scatter_dimension=0, tiled=True),
-        lax.psum_scatter(g_cbias, "row", scatter_dimension=0, tiled=True),
-        lax.psum_scatter(g_first, "row", scatter_dimension=0, tiled=True),
-        lax.psum_scatter(g_bfirst, "row", scatter_dimension=0, tiled=True),
-        lax.psum_scatter(g_second, "row", scatter_dimension=0, tiled=True),
-        lax.psum_scatter(g_bsecond, "row", scatter_dimension=0, tiled=True),
-        lax.psum_scatter(g_logit, "row", scatter_dimension=0, tiled=True),
-    )
-    s_down, s_up, s_cbias, s_first, s_bfirst, s_second, s_bsecond, s_logit = parted
-    totals = lax.psum(
-        (s_down, s_up, s_cbias, s_first, s_bfirst, s_second, s_bsecond, s_logit), "table"
-    )
-    return (
-        row_grads,
-        totals[0],
-        totals[1],
-        totals[2],
-        totals[3],
-        totals[4],
-        totals[5],
-        totals[6],
-        totals[7],
-    )
+    mine = jnp.transpose(lookup_slots[0]).reshape(hot_count, n_table, n_row, batch_dev)
+    mine = lax.dynamic_index_in_dim(mine, row_pos, axis=2, keepdims=False)
+    partial = scatter_rows(mine.reshape(-1), received.reshape(samples, width))
+    parts = partial.reshape(n_row, -1, width)
+    swapped = lax.all_to_all(parts, "row", split_axis=0, concat_axis=0, tiled=True)
+    row_grads = jnp.sum(swapped.astype(jnp.float32), axis=0)[None]
+    flat = jnp.concatenate([g.astype(jnp.bfloat16).reshape(n_row, -1) for g in grads], axis=1)
+    swapped = lax.all_to_all(flat, "row", split_axis=0, concat_axis=0, tiled=True)
+    total = lax.psum(jnp.sum(swapped.astype(jnp.float32), axis=0), "table")
+    outs = []
+    at = 0
+    for g in grads:
+        shape = (g.shape[0] // n_row,) + g.shape[1:]
+        size = g.size // n_row
+        outs.append(total[at : at + size].reshape(shape))
+        at += size
+    return (row_grads, *outs)
 
 
 def solution(mesh):

time: 1920 us -> 468 us (0.24)
  other arithmetic: 1400 us -> 54.4 us
  blocking collectives: 130 us -> 0 us
  waiting for transfers between devices: 330 us -> 206 us
  local copies, waits for them, and re-layouts: 18.4 us -> 118 us
  Pallas kernels: 0 us -> 29.3 us
  starting transfers between devices: 0.43 us -> 25.7 us
    scatter-add x4 -> x0, other arithmetic: 1400 us -> none  [local(): jax.ops.segment_sum(values, in_shard[0, :, which], num_segments=u_shard)]
    unnamed x9 -> x1, waiting for transfers between devices: 222 us -> 0.02 us
    psum x1, waiting for transfers between devices: 0.01 us -> 108 us  [local(): total = lax.psum(jnp.sum(swapped.astype(jnp.float32), axis=0), 'table')]
    all_to_all x0 -> x3, waiting for transfers between devices: none -> 97.9 us  [the longest x1 97.4 us: local(): lax.all_to_all(flat, 'row', split_axis=0, concat_axis=0, tiled=True)]
    reduce_scatter x1 -> x0, waiting for transfers between devices: 85.7 us -> none  [local(): lax.psum_scatter(g_second, 'row', scatter_dimension=0, tiled=True)]
    unnamed x54 -> x53, local copies, waits for them, and re-layouts: 15.1 us -> 94.8 us
    unnamed x1 -> x0, blocking collectives: 68 us -> none
    all_to_all x1 -> x0, blocking collectives: 35.9 us -> none  [local(): lax.all_to_all(pooled_grad, 'table', split_axis=1, concat_axis=0, tiled=T...]
  transfers between devices with their start and end apart: 6 -> 4, of which waited for: 5 -> 3; matrix products, arithmetic and copies ran while one was open for 74% -> 36% of each run, Pallas kernels for 0% -> 6%
where the time goes in v1:
time: 468 us; the launch traced here: 466 us
  waiting for transfers between devices  206 us (44%)
  local copies, waits for them, and re-layouts  118 us (25%)
  other arithmetic  54.4 us (12%)
  Pallas kernels  29.3 us (6%)
  starting transfers between devices  25.7 us (5%)
  matrix products  17.4 us (4%)
  between operations  14.3 us (3%)
    psum x1, waiting for transfers between devices, local(): total = lax.psum(jnp.sum(swapped.astype(jnp.float32), axis=0), 'table')  108 us
    all_to_all x1, waiting for transfers between devices, local(): lax.all_to_all(flat, 'row', split_axis=0, concat_axis=0, tiled=True)  97.4 us
    unnamed x53, local copies, waits for them, and re-layouts  94.8 us
    pallas_call x1, Pallas kernels, scatter_rows(): pl.pallas_call(scatter_kernel, out_shape=jax.ShapeDtypeStruct((total_slot...  29.3 us
    reduce_sum x1, other arithmetic, local(): total = lax.psum(jnp.sum(swapped.astype(jnp.float32), axis=0), 'table')  25.7 us
    all_to_all x1, other arithmetic, local(): lax.all_to_all(flat, 'row', split_axis=0, concat_axis=0, tiled=True)  22.9 us
    reshape x7, local copies, waits for them, and re-layouts, local(): g.astype(jnp.bfloat16).reshape(n_row, -1)  10.6 us
  transfers between devices with their start and end apart: 4, of which 3 were waited for; matrix products, arithmetic and copies ran while one was open for 36% of the time, Pallas kernels for 6%

profile of v1, /device:TPU:2, one launch (start us, length us, event | category | flops | bytes accessed | tf_op | source)
XLA Modules:
  0.0 465.7 jit_solution(14460546361544793214)
XLA Ops:
  13.4 1.7 fusion.4
  16.6 1.5 fusion.11
  20.4 8.8 %all-to-all-start = ((bf16[256,16,128]{2,0,1:T(8,128)(2,1)}), bf16[256,16,128]{2,0,1:T(8,128)(2,1)}, u32[]{:S(2)}, u32[]{:S(2)}) async-start(bf16[256,16,128]{2,0,1:T(8,128)(2,1)} %copy_bitcast_fusion), calls=%async_computation | async-start | bytes 2097152 | tf_op jit(solution)/shard_map/all_to_all | solution.py:166
  29.2 3.4 convolution_convert_fusion.3
  32.6 1.6 convolution_convert_fusion.1
  34.2 1.5 convolution_convert_fusion.2
  35.7 3.4 convolution_convert_fusion
  39.5 2.3 reshape.89
  43.3 1.6 reshape.84
  44.9 5.1 %reshape.87 = bf16[16,139264]{1,0:T(8,128)(2,1)} reshape(bf16[2176,1024]{1,0:T(8,128)(2,1)} %convolution_convert_fusion) | data formatting | bytes 8912896 | tf_op jit(solution)/shard_map/reshape | solution.py:173
  54.0 24.9 %dynamic-update-slice.3 = bf16[16,274760]{1,0:T(8,128)(2,1)} dynamic-update-slice(bf16[16,274760]{1,0:T(8,128)(2,1)} %dynamic-update-slice.2, bf16[16,139264]{1,0:T(8,128)(2,1)} %reshape.87, s32[]{} %constant.26, s32[]{} %constant.29) | dynamic-update-slice | bytes 8912900
  78.9 1.4 dynamic-update-slice.4
  80.4 12.0 %dynamic-update-slice.5 = bf16[16,274760]{1,0:T(8,128)(2,1)} dynamic-update-slice(bf16[16,274760]{1,0:T(8,128)(2,1)} %dynamic-update-slice.4, bf16[16,65536]{1,0:T(8,128)(2,1)S(1)} %reshape.89, s32[]{} %constant.26, s32[]{} %constant.31) | dynamic-update-slice | bytes 4194308
  92.4 1.4 dynamic-update-slice.6
  95.7 22.9 %reduce.4 = bf16[16,274760]{1,0:T(8,128)(2,1)} reduce(bf16[16,1,274760]{2,0,1:T(8,128)(2,1)} %bitcast.8, bf16[]{:T(256)} %broadcast.14), dimensions={1}, to_apply=%copy.24.reduce_sub_computation | reduce | bytes 17584642 | tf_op jit(solution)/shard_map/all_to_all | solution.py:174
  118.6 16.5 %reshape.95 = bf16[16,2,137380]{2,1,0:T(2,128)(2,1)} reshape(bf16[16,274760]{1,0:T(8,128)(2,1)} %reduce.4) | data formatting | bytes 17584640
  135.1 7.6 %all-to-all-start.2 = ((bf16[16,2,137380]{2,1,0:T(2,128)(2,1)}), bf16[16,2,137380]{2,1,0:T(2,128)(2,1)}, u32[]{:S(2)}, u32[]{:S(2)}) async-start(bf16[16,2,137380]{2,1,0:T(2,128)(2,1)} %reshape.95), calls=%async_computation.2 | async-start | bytes 17596416 | tf_op jit(solution)/shard_map/all_to_all | solution.py:174
  143.6 29.3 %shard_map.187 = bf16[16384,128]{1,0:T(8,128)(2,1)} custom-call(s32[16384]{0:T(1024)} %bitcast.44, bf16[4096,128]{1,0:T(8,128)(2,1)} %bitcast.5.v_ref), custom_call_target="tpu_custom_call" | custom-call | tf_op jit(solution)/shard_map/pallas_call | solution.py:120
  172.9 97.4 %all-to-all-done.2 = bf16[16,2,137380]{2,1,0:T(2,128)(2,1)} async-done(((bf16[16,2,137380]{2,1,0:T(2,128)(2,1)}), bf16[16,2,137380]{2,1,0:T(2,128)(2,1)}, u32[]{:S(2)}, u32[]{:S(2)}) %all-to-all-start.2) | async-done | bytes 8792352 | tf_op jit(solution)/shard_map/all_to_all | solution.py:174
  270.3 9.3 %all-to-all-start.1 = ((bf16[16,1024,128]{2,1,0:T(8,128)(2,1)}), bf16[16,1024,128]{2,1,0:T(8,128)(2,1)}, u32[]{:S(2)}, u32[]{:S(2)}) async-start(bf16[16,1024,128]{2,1,0:T(8,128)(2,1)} %bitcast.40), calls=%async_computation.1 | async-start | bytes 8388608 | tf_op jit(solution)/shard_map/all_to_all | solution.py:171
  279.6 31.9 %reshape.96 = bf16[16,1,274760]{2,1,0:T(2,128)(2,1)} reshape(bf16[16,2,137380]{2,1,0:T(2,128)(2,1)} %all-to-all-done.2) | data formatting | bytes 17584640
  311.5 25.7 %convert_reduce_fusion = f32[274760]{0:T(1024)} fusion(bf16[16,1,274760]{2,1,0:T(2,128)(2,1)} %reshape.96), kind=kLoop, calls=%fused_computation | loop fusion | flops 8517560 | bytes 9891360 | tf_op jit(solution)/shard_map/reduce_sum | solution.py:175
  337.8 3.7 convert_reduce_fusion.1
  341.6 108.3 %all-reduce.2.cloned.1.call-done = f32[274760]{0:T(1024)} async-done(((f32[274760]{0:T(1024)}), f32[274760]{0:T(1024)}) %all-reduce.2.cloned.1.call-update) | async-done | bytes 1099056 | tf_op jit(solution)/shard_map/psum | solution.py:175
  (79 shorter events, 28.1 us)
Async XLA Ops:
  7.2 6.2 %copy-start = (bf16[1024,1024]{1,0:T(8,128)(2,1)S(1)}, bf16[1024,1024]{1,0:T(8,128)(2,1)}, u32[]{:S(2)}) copy-start(bf16[1024,1024]{1,0:T(8,128)(2,1)} %param.20) | copy-start | bytes 6291460
  7.2 2.5 copy-start.8
  8.2 1.9 copy-start.5
  8.2 1.9 copy-start.15
  9.7 2.3 copy-start.4
  10.2 1.8 copy-start.18
  12.0 7.1 %copy-start.2 = (f32[256,2176]{1,0:T(8,128)}, f32[256,2176]{1,0:T(8,128)S(1)}, u32[]{:S(2)}) copy-start(f32[256,2176]{1,0:T(8,128)S(1)} %convolution_add_fusion) | copy-start | bytes 6684676
  12.0 1.4 copy-start.16
  12.0 1.4 copy-start.19
  13.4 2.2 copy-start.20
  13.4 1.8 copy-start.17
  16.6 1.5 copy-start.9
  20.4 8.8 %copy-start.14 = (bf16[256,1024]{1,0:T(8,128)(2,1)S(1)}, bf16[256,1024]{1,0:T(8,128)(2,1)}, u32[]{:S(2)}) copy-start(bf16[256,1024]{1,0:T(8,128)(2,1)} %copy-done.13) | copy-start | bytes 1572868
  20.4 114.7 %all-to-all-start = ((bf16[256,16,128]{2,0,1:T(8,128)(2,1)}), bf16[256,16,128]{2,0,1:T(8,128)(2,1)}, u32[]{:S(2)}, u32[]{:S(2)}) async-start(bf16[256,16,128]{2,0,1:T(8,128)(2,1)} %copy_bitcast_fusion), calls=%async_computation | async-start | bytes 2097152 | tf_op jit(solution)/shard_map/all_to_all | solution.py:166
  32.6 3.1 copy-start.3
  32.6 3.1 copy-start.10
  35.7 3.4 copy-start.12
  39.5 2.4 copy-start.6
  50.0 1.6 copy-start.7
  135.1 7.6 %copy-start.11 = (s32[1,65536,4]{1,2,0:T(4,128)S(1)}, s32[1,65536,4]{1,2,0:T(4,128)}, u32[]{:S(2)}) copy-start(s32[1,65536,4]{1,2,0:T(4,128)} %param.23) | copy-start | bytes 3145732
  135.1 135.2 %all-to-all-start.2 = ((bf16[16,2,137380]{2,1,0:T(2,128)(2,1)}), bf16[16,2,137380]{2,1,0:T(2,128)(2,1)}, u32[]{:S(2)}, u32[]{:S(2)}) async-start(bf16[16,2,137380]{2,1,0:T(2,128)(2,1)} %reshape.95), calls=%async_computation.2 | async-start | bytes 17596416 | tf_op jit(solution)/shard_map/all_to_all | solution.py:174
  270.3 67.6 %all-to-all-start.1 = ((bf16[16,1024,128]{2,1,0:T(8,128)(2,1)}), bf16[16,1024,128]{2,1,0:T(8,128)(2,1)}, u32[]{:S(2)}, u32[]{:S(2)}) async-start(bf16[16,1024,128]{2,1,0:T(8,128)(2,1)} %bitcast.40), calls=%async_computation.1 | async-start | bytes 8388608 | tf_op jit(solution)/shard_map/all_to_all | solution.py:171
  279.6 170.3 %all-reduce.2.cloned.1.call-start = ((), (), s32[]{:S(2)}) async-start(), calls=%async_computation.3 | async-start | bytes 2203648 | tf_op jit(solution)/shard_map/psum | solution.py:175
  337.8 121.0 %copy-start.1 = (bf16[1024,1024]{1,0:T(8,128)(2,1)S(1)}, bf16[1024,1024]{1,0:T(8,128)(2,1)}, u32[]{:S(2)}) copy-start(bf16[1024,1024]{1,0:T(8,128)(2,1)} %param.20) | copy-start | bytes 6291460
  (1 other events, 1.0 us)
Sparse Core Ops, SparseCore 0:
  337.4 112.4 all-reduce.1

commit v2 on v1

--- a/solution.py
+++ b/solution.py
@@ -13,7 +13,7 @@
     return sig * (1.0 + value * (1.0 - sig))
 
 
-def dense_backward(
+def dense_path(
     dense_feat,
     pooled,
     labels,
@@ -42,34 +42,503 @@
         jnp.bfloat16
     )
     grad_logit = jnp.sum(act_wide * delta_logit[:, None], axis=0)
-    grad_hidden2 = jnp.dot(act_first.T, delta_second, preferred_element_type=jnp.float32)
-    grad_bias2 = jnp.sum(delta_second.astype(jnp.float32), axis=0)
     back_first = jnp.dot(delta_second, w_hidden2.T, preferred_element_type=jnp.float32)
     delta_first = (back_first * swish_slope(pre_first)).astype(jnp.bfloat16)
-    grad_hidden1 = jnp.dot(crossed.T, delta_first, preferred_element_type=jnp.float32)
-    grad_bias1 = jnp.sum(delta_first.astype(jnp.float32), axis=0)
     delta_crossed = jnp.dot(delta_first, w_hidden1.T, preferred_element_type=jnp.float32)
     delta_widened = (delta_crossed * stacked_wide).astype(jnp.bfloat16)
-    grad_cross_up = jnp.dot(reduced.T, delta_widened, preferred_element_type=jnp.float32)
-    grad_cross_bias = jnp.sum(delta_widened.astype(jnp.float32), axis=0)
     delta_reduced = jnp.dot(delta_widened, cross_up.T, preferred_element_type=jnp.float32).astype(
         jnp.bfloat16
     )
-    grad_cross_down = jnp.dot(stacked.T, delta_reduced, preferred_element_type=jnp.float32)
     delta_stacked = delta_crossed * (widened + 1.0) + jnp.dot(
         delta_reduced, cross_down.T, preferred_element_type=jnp.float32
     )
-    grads = (
-        grad_cross_down,
-        grad_cross_up,
-        grad_cross_bias,
-        grad_hidden1,
-        grad_bias1,
-        grad_hidden2,
-        grad_bias2,
-        grad_logit,
-    )
-    return (grads, delta_stacked)
+    saved = (
+        stacked,
+        crossed,
+        reduced,
+        act_first,
+        delta_second,
+        delta_first,
+        delta_widened,
+        delta_reduced,
+        grad_logit[None, :],
+    )
+    return (saved, delta_stacked)
+
+
+MESH = pl.DeviceIdType.MESH
+X, Y, Z = 4, 4, 8
+PIECE = 144
+WIDE = 1024
+f32, bf16 = jnp.float32, jnp.bfloat16
+
+
+def place():
+    table = lax.axis_index("table")
+    row = lax.axis_index("row")
+    core, z = lax.rem(table, 2), table // 2
+    y, x = row // X, lax.rem(row, X)
+    return table, row, core, z, y, x
+
+
+def slot_of(half, shard, y, x):
+    dy = lax.rem(shard // X - y + Y, Y)
+    dx = lax.rem(lax.rem(shard, X) - x + X, X)
+    return dx * 4 + dy if half == 0 else dy * 4 + dx
+
+
+def shard_of(core, y, x, first, second):
+    dx = first * (1 - core) + second * core
+    dy = second * (1 - core) + first * core
+    return lax.rem(y + dy, Y) * X + lax.rem(x + dx, X)
+
+
+def transposed(dst, src):
+    def move(i, c):
+        at = pl.ds(pl.multiple_of(i * 128, 128), 128)
+        dst[at, :] = src[:, at].T
+        return c
+
+    lax.fori_loop(0, src.shape[1] // 128, move, 0)
+
+
+def weight_kernel(
+    stacked,
+    crossed,
+    reduced,
+    act_first,
+    delta_second,
+    delta_first,
+    delta_widened,
+    delta_reduced,
+    grad_logit,
+    out0,
+    out1,
+    out2,
+    out3,
+    packed,
+    landed,
+    flipped,
+    small,
+    send_sem,
+    recv_sem,
+):
+    table, row, core, z, y, x = place()
+    other = z * 2 + 1 - core
+    barrier = pltpu.get_barrier_semaphore()
+    pl.semaphore_signal(barrier, inc=1, device_id=(other, row), device_id_type=MESH)
+    pl.semaphore_wait(barrier, 1)
+
+    def copy(half, slot):
+        return pltpu.make_async_remote_copy(
+            src_ref=packed.at[half, slot],
+            dst_ref=landed.at[slot],
+            send_sem=send_sem.at[slot],
+            recv_sem=recv_sem.at[slot],
+            device_id=(other, row),
+            device_id_type=MESH,
+        )
+
+    def dot(a, b):
+        return jnp.dot(a, b, preferred_element_type=f32)
+
+    transposed(flipped, act_first)
+
+    def second(i, c):
+        m = dot(flipped[pl.ds(pl.multiple_of(i * 256, 256), 256), :], delta_second[...])
+        for k in range(4):
+            packed[1, slot_of(1, i * 4 + k, y, x), 0:64, :] = m[64 * k : 64 * k + 64].astype(bf16)
+        return c
+
+    lax.fori_loop(0, 4, second, 0)
+
+    transposed(small, reduced)
+
+    def up(i, c):
+        left = small[pl.ds(pl.multiple_of(i * 64, 64), 64), :]
+        m0 = dot(left, delta_widened[:, 0:1024])
+        m1 = dot(left, delta_widened[:, 1024:2048])
+        m2 = dot(left, delta_widened[:, 2048:2176])
+        for k in range(4):
+            slot = slot_of(1, i * 4 + k, y, x)
+            part = slice(16 * k, 16 * k + 16)
+            packed[1, slot, 64:80, :] = m0[part].astype(bf16)
+            packed[1, slot, 80:96, :] = m1[part].astype(bf16)
+            packed[1, slot, 96:112, 768:896] = m2[part].astype(bf16)
+            packed[1, slot, 96:112, 896:1024] = jnp.zeros((16, 128), bf16)
+            packed[1, slot, 128:144, 768:1024] = jnp.zeros((16, 256), bf16)
+        return c
+
+    lax.fori_loop(0, 4, up, 0)
+
+    transposed(flipped, stacked)
+
+    def down(i, c):
+        m = dot(flipped[pl.ds(pl.multiple_of(i * 272, 16), 272), :], delta_reduced[...])
+        for k in range(2):
+            slot = slot_of(1, i * 2 + k, y, x)
+            d = m[136 * k : 136 * k + 136]
+            packed[1, slot, 96:144, 0:256] = d[0:48].astype(bf16)
+            packed[1, slot, 96:144, 256:512] = d[48:96].astype(bf16)
+            last = jnp.concatenate([d[96:136], jnp.zeros((8, 256), f32)], axis=0)
+            packed[1, slot, 96:144, 512:768] = last.astype(bf16)
+        return c
+
+    lax.fori_loop(0, 8, down, 0)
+
+    ones = jnp.ones((8, 256), bf16)
+    wide_sums = dot(ones, delta_widened[...])
+    which = lax.broadcasted_iota(jnp.int32, (8, 1024), 0)
+    sums = jnp.where(which == 1, dot(ones, delta_first[...]), dot(ones, delta_second[...]))
+    sums = jnp.where(which == 3, grad_logit[...], sums)
+    first_row = which[:, 0:256] == 0
+    for shard in range(16):
+        a = wide_sums if shard == 0 else pltpu.roll(wide_sums, 2176 - 136 * shard, 1)
+        b = sums if shard == 0 else pltpu.roll(sums, 1024 - 64 * shard, 1)
+        block = jnp.where(first_row, a[:, 0:256], b[:, 0:256])
+        block = jnp.concatenate([block, jnp.zeros((8, 256), f32)], axis=0).astype(bf16)
+        packed[1, slot_of(1, shard, y, x), 112:128, 768:1024] = block
+
+    @pl.when(core == 0)
+    def _():
+        def send(slot, c):
+            copy(1, slot).start()
+            return c
+
+        lax.fori_loop(0, 16, send, 0)
+
+    transposed(flipped, crossed)
+
+    def first(i, c):
+        m = dot(flipped[pl.ds(pl.multiple_of(i * 272, 16), 272), :], delta_first[...])
+        for k in range(2):
+            slot = slot_of(0, i * 2 + k, y, x)
+            d = jnp.concatenate([m[136 * k : 136 * k + 136], jnp.zeros((8, WIDE), f32)], axis=0)
+            packed[0, slot] = d.astype(bf16)
+
+            @pl.when(core == 1)
+            def _():
+                copy(0, slot).start()
+
+        return c
+
+    lax.fori_loop(0, 8, first, 0)
+
+    for shift, out in enumerate((out0, out1, out2, out3)):
+
+        def add(i, c):
+            slot = shift * 4 + i
+            copy(1 - core, slot).wait_recv()
+            out[i] = (packed[core, slot].astype(f32) + landed[slot].astype(f32)).astype(bf16)
+            return c
+
+        lax.fori_loop(0, 4, add, 0)
+
+    def drain(slot, c):
+        copy(1 - core, slot).wait_send()
+        return c
+
+    lax.fori_loop(0, 16, drain, 0)
+
+
+def weight_grads(saved):
+    vmem = pl.BlockSpec(memory_space=pltpu.VMEM)
+    piece = jax.ShapeDtypeStruct((4, PIECE, WIDE), bf16)
+    return pl.pallas_call(
+        weight_kernel,
+        out_shape=(piece,) * 4,
+        in_specs=[vmem] * 9,
+        out_specs=(vmem,) * 4,
+        scratch_shapes=[
+            pltpu.VMEM((2, 16, PIECE, WIDE), bf16),
+            pltpu.VMEM((16, PIECE, WIDE), bf16),
+            pltpu.VMEM((2176, 256), bf16),
+            pltpu.VMEM((256, 256), bf16),
+            pltpu.SemaphoreType.DMA((16,)),
+            pltpu.SemaphoreType.DMA((16,)),
+        ],
+        compiler_params=pltpu.CompilerParams(
+            collective_id=0, has_side_effects=True, vmem_limit_bytes=48 << 20
+        ),
+        cost_estimate=pl.CostEstimate(
+            flops=2_300_000_000, bytes_accessed=60_000_000, transcendentals=0
+        ),
+    )(*saved)
+
+
+def exchange_kernel(
+    parts,
+    s0,
+    s1,
+    s2,
+    s3,
+    row_out,
+    h1_out,
+    h2_out,
+    up_out,
+    down_out,
+    vec_out,
+    own,
+    got1,
+    mid,
+    got2,
+    dense,
+    dense_mid,
+    dense_got,
+    zparts,
+    zgot,
+    final,
+    local_sem,
+    send1,
+    recv1,
+    send2,
+    recv2,
+    wsend,
+    wrecv,
+    zsend,
+    zrecv,
+    gsend,
+    grecv,
+    csend,
+    crecv,
+):
+    table, row, core, z, y, x = place()
+    sibling = z * 2 + 1 - core
+
+    def first_peer(d):
+        return (table, shard_of(core, y, x, d, 0))
+
+    def second_peer(j):
+        return (table, shard_of(core, y, x, 0, j))
+
+    def z_peer(d):
+        return (lax.rem(z + d, Z) * 2 + core, row)
+
+    def remote(src, dst, s, r, who):
+        return pltpu.make_async_remote_copy(
+            src_ref=src, dst_ref=dst, send_sem=s, recv_sem=r, device_id=who, device_id_type=MESH
+        )
+
+    barrier = pltpu.get_barrier_semaphore()
+    peers = [first_peer(d) for d in (1, 2, 3)] + [second_peer(j) for j in (1, 2, 3)]
+    peers += [z_peer(d) for d in range(1, Z)] + [(sibling, row)]
+    for who in peers:
+        pl.semaphore_signal(barrier, inc=1, device_id=who, device_id_type=MESH)
+    pl.semaphore_wait(barrier, len(peers))
+
+    def copy1(d, j):
+        return remote(
+            parts.at[shard_of(core, y, x, d, j)],
+            got1.at[d - 1, j],
+            send1.at[d - 1, j],
+            recv1.at[d - 1, j],
+            first_peer(d),
+        )
+
+    def copy2(j):
+        return remote(mid.at[j - 1], got2.at[j - 1], send2.at[j - 1], recv2.at[j - 1], second_peer(j))
+
+    def copyw(j):
+        return remote(
+            dense_mid.at[j - 1], dense_got.at[j - 1], wsend.at[j - 1], wrecv.at[j - 1], second_peer(j)
+        )
+
+    def copyz(d):
+        return remote(
+            zparts.at[lax.rem(z + d, Z)], zgot.at[d - 1], zsend.at[d - 1], zrecv.at[d - 1], z_peer(d)
+        )
+
+    def copyg(d, which):
+        piece = final.at[core, which]
+        return remote(piece, piece, gsend.at[d - 1], grecv.at[d - 1], z_peer(d))
+
+    def copyc(half):
+        return remote(final.at[half], final.at[half], csend, crecv, (sibling, row))
+
+    def local_dense(d):
+        return pltpu.make_async_copy((s0, s1, s2, s3)[d], dense.at[d], local_sem.at[d])
+
+    def local_own(j):
+        return pltpu.make_async_copy(
+            parts.at[shard_of(core, y, x, 0, j)], own.at[j], local_sem.at[4 + j]
+        )
+
+    for d in range(4):
+        local_dense(d).start()
+    for j in (1, 2, 3, 0):
+        for d in (1, 2, 3):
+            copy1(d, j).start()
+    for j in range(4):
+        local_own(j).start()
+    for d in range(4):
+        local_dense(d).wait()
+
+    def dense_sum(j, at):
+        total = dense[0, j, at, :].astype(f32)
+        for d in (1, 2, 3):
+            total = total + dense[d, j, at, :].astype(f32)
+        return total
+
+    for j in (1, 2, 3):
+
+        def dense_block(i, c):
+            at = pl.ds(pl.multiple_of(i * 16, 16), 16)
+            dense_mid[j - 1, at, :] = dense_sum(j, at).astype(bf16)
+            return c
+
+        lax.fori_loop(0, PIECE // 16, dense_block, 0)
+        copyw(j).start()
+    for j in range(4):
+        local_own(j).wait()
+    for j in (1, 2, 3):
+        copyw(j).wait_recv()
+
+    def dense_last(i, c):
+        at = pl.ds(pl.multiple_of(i * 16, 16), 16)
+        total = dense_sum(0, at)
+        for j in (1, 2, 3):
+            total = total + dense_got[j - 1, at, :].astype(f32)
+        total = total.astype(bf16)
+        for k in range(Z):
+            zparts[k, at, :] = total[:, 128 * k : 128 * k + 128]
+        return c
+
+    lax.fori_loop(0, PIECE // 16, dense_last, 0)
+    for d in range(1, Z):
+        copyz(d).start()
+
+    def row_sum(j, at):
+        total = own[j, at, :].astype(f32)
+        for d in (1, 2, 3):
+            total = total + got1[d - 1, j, at, :].astype(f32)
+        return total
+
+    def row_mid(j):
+        for d in (1, 2, 3):
+            copy1(d, j).wait_recv()
+
+        def block(i, c):
+            at = pl.ds(pl.multiple_of(i * 128, 128), 128)
+            mid[j - 1, at, :] = row_sum(j, at).astype(bf16)
+            return c
+
+        lax.fori_loop(0, 8, block, 0)
+        copy2(j).start()
+
+    row_mid(1)
+    for d in range(1, Z):
+        copyz(d).wait_recv()
+    total = zparts[z].astype(f32)
+    for d in range(1, Z):
+        total = total + zgot[d - 1].astype(f32)
+    final[core, z] = total.astype(bf16)
+    for d in range(1, Z):
+        copyg(d, z).start()
+    row_mid(2)
+    for d in range(1, Z):
+        copyg(d, lax.rem(z - d + Z, Z)).wait_recv()
+    copyc(core).start()
+    row_mid(3)
+    for d in (1, 2, 3):
+        copy1(d, 0).wait_recv()
+    copyc(1 - core).wait_recv()
+    for k in range(Z):
+        at = slice(128 * k, 128 * k + 128)
+        h1_out[:, at] = final[0, k, :, :].astype(f32)[0:136]
+        h2_out[:, at] = final[1, k, 0:64, :].astype(f32)
+        up_out[:, at] = final[1, k, 64:80, :].astype(f32)
+        up_out[:, 1024 + 128 * k : 1024 + 128 * k + 128] = final[1, k, 80:96, :].astype(f32)
+    up_out[:, 2048:2176] = final[1, 6, 96:112, :].astype(f32)
+    for k in range(2):
+        at = slice(128 * k, 128 * k + 128)
+        down_out[0:48, at] = final[1, k, 96:144, :].astype(f32)
+        down_out[48:96, at] = final[1, 2 + k, 96:144, :].astype(f32)
+        down_out[96:136, at] = final[1, 4 + k, 96:144, :].astype(f32)[0:40]
+        vec_out[:, at] = final[1, 6 + k, 112:128, :].astype(f32)[0:8]
+    for j in (1, 2, 3):
+        copy2(j).wait_recv()
+
+    def row_last(i, c):
+        at = pl.ds(pl.multiple_of(i * 128, 128), 128)
+        total = row_sum(0, at)
+        for j in (1, 2, 3):
+            total = total + got2[j - 1, at, :].astype(f32)
+        row_out[at, :] = total
+        return c
+
+    lax.fori_loop(0, 8, row_last, 0)
+
+    for d in (1, 2, 3):
+        for j in range(4):
+            copy1(d, j).wait_send()
+    for j in (1, 2, 3):
+        copy2(j).wait_send()
+        copyw(j).wait_send()
+    for d in range(1, Z):
+        copyz(d).wait_send()
+        copyg(d, z).wait_send()
+    copyc(core).wait_send()
+
+
+def exchange(parts, sums):
+    vmem = pl.BlockSpec(memory_space=pltpu.VMEM)
+    anywhere = pl.BlockSpec(memory_space=pl.ANY)
+    rows, width = parts.shape[1:]
+    dma = pltpu.SemaphoreType.DMA
+    return pl.pallas_call(
+        exchange_kernel,
+        out_shape=(
+            jax.ShapeDtypeStruct((rows, width), f32),
+            jax.ShapeDtypeStruct((136, 1024), f32),
+            jax.ShapeDtypeStruct((64, 1024), f32),
+            jax.ShapeDtypeStruct((16, 2176), f32),
+            jax.ShapeDtypeStruct((136, 256), f32),
+            jax.ShapeDtypeStruct((8, 256), f32),
+        ),
+        in_specs=[anywhere] * 5,
+        out_specs=(vmem,) * 6,
+        scratch_shapes=[
+            pltpu.VMEM((4, rows, width), bf16),
+            pltpu.VMEM((3, 4, rows, width), bf16),
+            pltpu.VMEM((3, rows, width), bf16),
+            pltpu.VMEM((3, rows, width), bf16),
+            pltpu.VMEM((4, 4, PIECE, WIDE), bf16),
+            pltpu.VMEM((3, PIECE, WIDE), bf16),
+            pltpu.VMEM((3, PIECE, WIDE), bf16),
+            pltpu.VMEM((Z, PIECE, 128), bf16),
+            pltpu.VMEM((Z - 1, PIECE, 128), bf16),
+            pltpu.VMEM((2, Z, PIECE, 128), bf16),
+            dma((8,)),
+            dma((3, 4)),
+            dma((3, 4)),
+            dma((3,)),
+            dma((3,)),
+            dma((3,)),
+            dma((3,)),
+            dma((Z - 1,)),
+            dma((Z - 1,)),
+            dma((Z - 1,)),
+            dma((Z - 1,)),
+            dma,
+            dma,
+        ],
+        compiler_params=pltpu.CompilerParams(
+            collective_id=1, has_side_effects=True, vmem_limit_bytes=48 << 20
+        ),
+    )(parts, *sums)
+
+
+def first_axis_pairs(shift):
+    pairs = []
+    for table in range(2 * Z):
+        for row in range(Y * X):
+            y, x = row // X, row % X
+            if table % 2 == 0:
+                x = (x + shift) % X
+            else:
+                y = (y + shift) % Y
+            pairs.append((table * Y * X + row, table * Y * X + y * X + x))
+    return pairs
 
 
 def scatter_kernel(s_ref, v_ref, o_ref, wide, *accs):
@@ -125,6 +594,9 @@
         scratch_shapes=[pltpu.VMEM((count, width), jnp.float32)]
         + [pltpu.VMEM((total_slots, width), jnp.float32)] * (slots.size // count),
         compiler_params=pltpu.CompilerParams(vmem_limit_bytes=58 << 20),
+        cost_estimate=pl.CostEstimate(
+            flops=10_000_000, bytes_accessed=100_000_000, transcendentals=0
+        ),
     )(slots, values)
 
 
@@ -142,7 +614,7 @@
     w_logit,
     lookup_slots,
 ):
-    grads, delta_stacked = dense_backward(
+    saved, delta_stacked = dense_path(
         dense_feat,
         pooled,
         labels,
@@ -163,24 +635,30 @@
     samples = n_table * batch_dev
     row_pos = lax.axis_index("row")
     pooled_grad = delta_stacked[:, width:].astype(jnp.bfloat16).reshape(batch_dev, n_table, width)
+    saved, pooled_grad = lax.optimization_barrier((saved, pooled_grad))
     received = lax.all_to_all(pooled_grad, "table", split_axis=1, concat_axis=0, tiled=True)
     mine = jnp.transpose(lookup_slots[0]).reshape(hot_count, n_table, n_row, batch_dev)
     mine = lax.dynamic_index_in_dim(mine, row_pos, axis=2, keepdims=False)
+    kept, *away = weight_grads(saved)
+    came = [
+        lax.ppermute(part, ("table", "row"), first_axis_pairs(shift + 1))
+        for shift, part in enumerate(away)
+    ]
     partial = scatter_rows(mine.reshape(-1), received.reshape(samples, width))
-    parts = partial.reshape(n_row, -1, width)
-    swapped = lax.all_to_all(parts, "row", split_axis=0, concat_axis=0, tiled=True)
-    row_grads = jnp.sum(swapped.astype(jnp.float32), axis=0)[None]
-    flat = jnp.concatenate([g.astype(jnp.bfloat16).reshape(n_row, -1) for g in grads], axis=1)
-    swapped = lax.all_to_all(flat, "row", split_axis=0, concat_axis=0, tiled=True)
-    total = lax.psum(jnp.sum(swapped.astype(jnp.float32), axis=0), "table")
-    outs = []
-    at = 0
-    for g in grads:
-        shape = (g.shape[0] // n_row,) + g.shape[1:]
-        size = g.size // n_row
-        outs.append(total[at : at + size].reshape(shape))
-        at += size
-    return (row_grads, *outs)
+    row_grads, g_h1, g_h2, g_up, g_down, vecs = exchange(
+        partial.reshape(n_row, -1, width), [kept] + came
+    )
+    return (
+        row_grads[None],
+        g_down,
+        g_up,
+        vecs[0, 0:136],
+        g_h1,
+        vecs[1, 0:64],
+        g_h2,
+        vecs[2, 0:64],
+        vecs[3, 0:64],
+    )
 
 
 def solution(mesh):

time: 468 us -> 146 us (0.31)
  waiting for transfers between devices: 206 us -> 0.01 us
  local copies, waits for them, and re-layouts: 118 us -> 22.4 us
  Pallas kernels: 29.3 us -> 99.8 us
  other arithmetic: 54.4 us -> 0.85 us
  between operations: 14.3 us -> 0.93 us
  starting transfers between devices: 25.7 us -> 14 us
  matrix products: 17.4 us -> 6.88 us
    psum x1 -> x0, waiting for transfers between devices: 108 us -> none  [local(): total = lax.psum(jnp.sum(swapped.astype(jnp.float32), axis=0), 'table')]
    all_to_all x2 -> x0, waiting for transfers between devices: 97.9 us -> none  [the longest x1 97.4 us: local(): lax.all_to_all(flat, 'row', split_axis=0, concat_axis=0, tiled=True)]
    unnamed x53 -> x48, local copies, waits for them, and re-layouts: 94.8 us -> 17.1 us
    pallas_call x0 -> x2, Pallas kernels: none -> 70.6 us  [the longest x1 51.7 us: exchange(): pl.pallas_call(exchange_kernel, out_shape=(jax.ShapeDtypeStruct((rows, wi...]
    reduce_sum x4 -> x1, other arithmetic: 30.1 us -> 0.5 us  [dense_path(): grad_logit = jnp.sum(act_wide * delta_logit[:, None], axis=0)]
    all_to_all x1 -> x0, other arithmetic: 22.9 us -> none  [local(): lax.all_to_all(flat, 'row', split_axis=0, concat_axis=0, tiled=True)]
    all_to_all x2 -> x0, starting transfers between devices: 16.9 us -> none  [the longest x1 9.29 us: local(): lax.all_to_all(parts, 'row', split_axis=0, concat_axis=0, tiled=True)]
    reshape x11 -> x0, local copies, waits for them, and re-layouts: 13.6 us -> none  [the longest x7 10.6 us: local(): g.astype(jnp.bfloat16).reshape(n_row, -1)]
  transfers between devices with their start and end apart: 4 -> 4, of which waited for: 3 -> 0; matrix products, arithmetic and copies ran while one was open for 36% -> 3% of each run, Pallas kernels for 6% -> 33%
where the time goes in v2:
time: 146 us; the launch traced here: 145 us
  Pallas kernels  99.8 us (68%)
  local copies, waits for them, and re-layouts  22.4 us (15%)
  starting transfers between devices  14 us (10%)
  matrix products  6.88 us (5%)
    pallas_call x1, Pallas kernels, exchange(): pl.pallas_call(exchange_kernel, out_shape=(jax.ShapeDtypeStruct((rows, wi...  51.7 us
    pallas_call x1, Pallas kernels, scatter_rows(): pl.pallas_call(scatter_kernel, out_shape=jax.ShapeDtypeStruct((total_slot...  29.2 us
    pallas_call x1, Pallas kernels, weight_grads(): pl.pallas_call(weight_kernel, out_shape=(piece,) * 4, in_specs=[vmem] * 9...  18.9 us
    unnamed x48, local copies, waits for them, and re-layouts  17.1 us
    all_to_all x1, starting transfers between devices, local(): lax.all_to_all(pooled_grad, 'table', split_axis=1, concat_axis=0, tiled=T...  8.63 us
    ppermute x3, starting transfers between devices, local(): lax.ppermute(part, ('table', 'row'), first_axis_pairs(shift + 1))  5.41 us
  transfers between devices with their start and end apart: 4, of which 0 were waited for; matrix products, arithmetic and copies ran while one was open for 3% of the time, Pallas kernels for 33%

profile of v2, /device:TPU:2, one launch (start us, length us, event | category | flops | bytes accessed | tf_op | source)
XLA Modules:
  0.0 145.0 jit_solution(16789103420655103750)
XLA Ops:
  0.7 1.0 constant_dynamic-update-slice_fusion.1
  1.7 1.3 constant_dynamic-update-slice_fusion.stacked
  4.8 2.1 %copy-done.13 = bf16[2176,1024]{1,0:T(8,128)(2,1)S(1)} copy-done((bf16[2176,1024]{1,0:T(8,128)(2,1)S(1)}, bf16[2176,1024]{1,0:T(8,128)(2,1)}, u32[]{:S(2)}) %copy-start.13) | copy-done | bytes 4456472
  6.9 1.6 %multiply_convert_fusion.2 = (bf16[256,1024]{1,0:T(8,128)(2,1)S(1)}, f32[256,1024]{1,0:T(8,128)S(1)}) fusion(f32[1024]{0:T(1024)S(1)} %copy-done.18, bf16[256,2176]{1,0:T(8,128)(2,1)S(1)} %get-tuple-element.31.crossed, bf16[2176,1024]{1,0:T(8,128)(2,1)S(1)} %copy-done.13), kind=kOutput, calls=%fused_computation.23 | convolution fusion | flops 1142423552 | bytes 7147520 | tf_op jit(solution)/shard_map/dot_general | solution.py:34
  8.6 1.0 fusion.4
  10.1 0.9 fusion.3.delta_first
  11.8 1.4 fusion
  15.3 1.3 copy.22
  16.6 8.6 %all-to-all-start = ((bf16[256,16,128]{2,0,1:T(8,128)(2,1)}), bf16[256,16,128]{2,0,1:T(8,128)(2,1)}, u32[]{:S(2)}, u32[]{:S(2)}) async-start(bf16[256,16,128]{2,0,1:T(8,128)(2,1)} %copy.22), calls=%async_computation | async-start | bytes 2097152 | tf_op jit(solution)/shard_map/all_to_all | solution.py:639
  25.2 1.2 copy-done.2
  26.4 1.2 copy-done.5
  27.7 1.0 copy-done.7
  28.7 1.0 copy-done.9
  29.8 1.0 copy-done.11
  30.8 18.9 %shard_map.188 = (bf16[4,144,1024]{2,1,0:T(8,128)(2,1)}, bf16[4,144,1024]{2,1,0:T(8,128)(2,1)}, bf16[4,144,1024]{2,1,0:T(8,128)(2,1)}, bf16[4,144,1024]{2,1,0:T(8,128)(2,1)}) custom-call(bf16[256,2176]{1,0:T(8,128)(2,1)S(1)} %constant_dynamic-update-slice_fusion.stacked, bf16[256,2176]{1,0:T(8,128)(2,1)S(1)} %copy-done.5, ...), custom_call_target="tpu_custom_call" | custom-call | flops 2300000000 | bytes 60000000 | tf_op jit(solution)/shard_map/pallas_call | solution.py:247
  49.7 1.8 %collective-permute-start = (bf16[4,144,1024]{2,1,0:T(8,128)(2,1)}, bf16[4,144,1024]{2,1,0:T(8,128)(2,1)S(1)}, u32[]{:S(2)}, u32[]{:S(2)}) collective-permute-start(bf16[4,144,1024]{2,1,0:T(8,128)(2,1)} %get-tuple-element.40), channel_id=1, source_target_pairs={{0,1},{1,2},{2,3},{3,0},{4,5},{5,6},{6,7},{7,4},{8,9},{9,10},{10,1... | collective-permute-start | bytes 3538952 | tf_op jit(solution)/shard_map/ppermute | solution.py:644
  51.6 1.0 collective-permute-start.1
  52.6 2.5 %collective-permute-start.2 = (bf16[4,144,1024]{2,1,0:T(8,128)(2,1)}, bf16[4,144,1024]{2,1,0:T(8,128)(2,1)}, u32[]{:S(2)}, u32[]{:S(2)}) collective-permute-start(bf16[4,144,1024]{2,1,0:T(8,128)(2,1)} %get-tuple-element.42), channel_id=1, source_target_pairs={{0,3},{1,0},{2,1},{3,2},{4,7},{5,4},{6,5},{7,6},{8,11},{9,8},{10,9... | collective-permute-start | bytes 3538952 | tf_op jit(solution)/shard_map/ppermute | solution.py:644
  55.1 2.4 %copy.23 = s32[1,4,256,256]{3,2,1,0:T(8,128)} copy(s32[1,4,256,256]{3,1,2,0:T(4,128)} %bitcast.46) | data formatting | bytes 2097152
  57.6 1.7 %constant_dynamic-slice_fusion = s32[4,16,1,256]{3,2,1,0:T(1,128)} fusion(s32[4,16,16,256]{3,2,1,0:T(8,128)} %bitcast.45, s32[]{:T(128)S(6)} %select_n.4), kind=kLoop, calls=%fused_computation.32 | loop fusion | bytes 131076 | tf_op jit(solution)/shard_map/jit(dynamic_index_in_dim)/dynamic_slice | solution.py:641
  59.3 29.2 %shard_map.187 = bf16[16384,128]{1,0:T(8,128)(2,1)} custom-call(s32[16384]{0:T(1024)} %bitcast.47, bf16[4096,128]{1,0:T(8,128)(2,1)} %bitcast.6.v_ref), custom_call_target="tpu_custom_call" | custom-call | flops 10000000 | bytes 100000000 | tf_op jit(solution)/shard_map/pallas_call | solution.py:589
  88.6 51.7 %shard_map.189 = (f32[1024,128]{1,0:T(8,128)S(1)}, f32[136,1024]{1,0:T(8,128)S(1)}, f32[64,1024]{1,0:T(8,128)S(1)}, f32[16,2176]{1,0:T(8,128)S(1)}, f32[136,256]{1,0:T(8,128)S(1)}, /*index=5*/f32[8,256]{1,0:T(8,128)S(1)}) custom-call(bf16[16,1024,128]{2,1,0:T(8,128)(2,1)} %bitcast.43, bf16[4,144,1024]{2,1,0:T(8,128)(2,1)S(1)} %copy-done.3, ...), custom_call_target="tpu_custom_call" | custom-call | tf_op jit(solution)/shard_map/pallas_call | solution.py:488
  141.3 0.8 copy.31
  143.5 0.8 copy.34
  (51 shorter events, 8.3 us)
Async XLA Ops:
  0.6 7.9 %copy-start = (bf16[1024,1024]{1,0:T(8,128)(2,1)S(1)}, bf16[1024,1024]{1,0:T(8,128)(2,1)}, u32[]{:S(2)}) copy-start(bf16[1024,1024]{1,0:T(8,128)(2,1)} %param.20) | copy-start | bytes 6291460
  0.7 2.3 %copy-start.14 = (bf16[2176,256]{1,0:T(8,128)(2,1)S(1)}, bf16[2176,256]{1,0:T(8,128)(2,1)}, u32[]{:S(2)}) copy-start(bf16[2176,256]{1,0:T(8,128)(2,1)} %param.15) | copy-start | bytes 3342340
  3.0 1.3 copy-start.12
  3.0 1.2 copy-start.15
  4.3 2.7 %copy-start.13 = (bf16[2176,1024]{1,0:T(8,128)(2,1)S(1)}, bf16[2176,1024]{1,0:T(8,128)(2,1)}, u32[]{:S(2)}) copy-start(bf16[2176,1024]{1,0:T(8,128)(2,1)} %param.18) | copy-start | bytes 13369348
  4.3 2.7 %copy-start.18 = (f32[1024]{0:T(1024)S(1)}, f32[1024]{0:T(1024)}, u32[]{:S(2)}) copy-start(f32[1024]{0:T(1024)} %param.19) | copy-start | bytes 12292
  4.8 3.7 %copy-start.4 = (bf16[256,2176]{1,0:T(8,128)(2,1)}, bf16[256,2176]{1,0:T(8,128)(2,1)S(1)}, u32[]{:S(2)}) copy-start(bf16[256,2176]{1,0:T(8,128)(2,1)S(1)} %get-tuple-element.31.crossed) | copy-start | bytes 3342340
  6.9 1.6 %copy-start.16 = (f32[1024]{0:T(1024)S(1)}, f32[1024]{0:T(1024)}, u32[]{:S(2)}) copy-start(f32[1024]{0:T(1024)} %param.22) | copy-start | bytes 12292
  6.9 1.6 %copy-start.19 = (f32[1024]{0:T(1024)S(1)}, f32[1024]{0:T(1024)}, u32[]{:S(2)}) copy-start(f32[1024]{0:T(1024)} %param.21) | copy-start | bytes 12292
  8.5 1.1 copy-start.10
  8.6 1.0 copy-start.17
  11.0 0.8 copy-start.8
  11.8 1.4 copy-start.6
  13.2 1.0 copy-start.1
  16.6 42.7 %all-to-all-start = ((bf16[256,16,128]{2,0,1:T(8,128)(2,1)}), bf16[256,16,128]{2,0,1:T(8,128)(2,1)}, u32[]{:S(2)}, u32[]{:S(2)}) async-start(bf16[256,16,128]{2,0,1:T(8,128)(2,1)} %copy.22), calls=%async_computation | async-start | bytes 2097152 | tf_op jit(solution)/shard_map/all_to_all | solution.py:639
  25.2 1.2 copy-start.2
  26.4 1.2 copy-start.5
  27.7 1.0 copy-start.7
  28.7 1.0 copy-start.9
  29.8 1.0 copy-start.11
  49.7 38.8 %collective-permute-start = (bf16[4,144,1024]{2,1,0:T(8,128)(2,1)}, bf16[4,144,1024]{2,1,0:T(8,128)(2,1)S(1)}, u32[]{:S(2)}, u32[]{:S(2)}) collective-permute-start(bf16[4,144,1024]{2,1,0:T(8,128)(2,1)} %get-tuple-element.40), channel_id=1, source_target_pairs={{0,1},{1,2},{2,3},{3,0},{4,5},{5,6},{6,7},{7,4},{8,9},{9,10},{10,1... | collective-permute-start | bytes 3538952 | tf_op jit(solution)/shard_map/ppermute | solution.py:644
  51.6 37.0 %collective-permute-start.1 = (bf16[4,144,1024]{2,1,0:T(8,128)(2,1)}, bf16[4,144,1024]{2,1,0:T(8,128)(2,1)}, u32[]{:S(2)}, u32[]{:S(2)}) collective-permute-start(bf16[4,144,1024]{2,1,0:T(8,128)(2,1)} %get-tuple-element.41), channel_id=1, source_target_pairs={{0,2},{1,3},{2,0},{3,1},{4,6},{5,7},{6,4},{7,5},{8,10},{9,11},{10,... | collective-permute-start | bytes 3538952 | tf_op jit(solution)/shard_map/ppermute | solution.py:644
  52.6 36.0 %collective-permute-start.2 = (bf16[4,144,1024]{2,1,0:T(8,128)(2,1)}, bf16[4,144,1024]{2,1,0:T(8,128)(2,1)}, u32[]{:S(2)}, u32[]{:S(2)}) collective-permute-start(bf16[4,144,1024]{2,1,0:T(8,128)(2,1)} %get-tuple-element.42), channel_id=1, source_target_pairs={{0,3},{1,0},{2,1},{3,2},{4,7},{5,4},{6,5},{7,6},{8,11},{9,8},{10,9... | collective-permute-start | bytes 3538952 | tf_op jit(solution)/shard_map/ppermute | solution.py:644
  59.3 29.3 %copy-start.3 = (bf16[4,144,1024]{2,1,0:T(8,128)(2,1)S(1)}, bf16[4,144,1024]{2,1,0:T(8,128)(2,1)}, u32[]{:S(2)}) copy-start(bf16[4,144,1024]{2,1,0:T(8,128)(2,1)} %get-tuple-element.39.s0) | copy-start | bytes 3538948

commit v3 on v2

--- a/solution.py
+++ b/solution.py
@@ -278,12 +278,19 @@
     up_out,
     down_out,
     vec_out,
-    own,
-    got1,
+    via_plus,
+    via_minus,
+    acc_plus,
+    acc_minus,
+    got_plus,
+    got_minus,
     mid,
+    via2,
     got2,
     dense,
     dense_mid,
+    dense_via_plus,
+    dense_via_minus,
     dense_got,
     zparts,
     zgot,
@@ -304,6 +311,7 @@
 ):
     table, row, core, z, y, x = place()
     sibling = z * 2 + 1 - core
+    rows = parts.shape[1]
 
     def first_peer(d):
         return (table, shard_of(core, y, x, d, 0))
@@ -320,28 +328,82 @@
         )
 
     barrier = pltpu.get_barrier_semaphore()
-    peers = [first_peer(d) for d in (1, 2, 3)] + [second_peer(j) for j in (1, 2, 3)]
+    peers = [first_peer(1), first_peer(3), second_peer(1), second_peer(3)]
     peers += [z_peer(d) for d in range(1, Z)] + [(sibling, row)]
     for who in peers:
         pl.semaphore_signal(barrier, inc=1, device_id=who, device_id_type=MESH)
     pl.semaphore_wait(barrier, len(peers))
 
-    def copy1(d, j):
-        return remote(
-            parts.at[shard_of(core, y, x, d, j)],
-            got1.at[d - 1, j],
-            send1.at[d - 1, j],
-            recv1.at[d - 1, j],
-            first_peer(d),
+    def ring(chunk, cut, size, vias, accs, gots, send, recv, plus, minus):
+        low, high = pl.ds(0, cut), pl.ds(cut, size - cut)
+        pairs = (
+            (chunk(2).at[low], vias[0], plus),
+            (chunk(2).at[high], vias[1], minus),
+            (chunk(1).at[high], gots[0].at[high], plus),
+            (chunk(3).at[low], gots[1].at[low], minus),
+            (accs[0], gots[0].at[low], plus),
+            (accs[1], gots[1].at[high], minus),
         )
 
-    def copy2(j):
-        return remote(mid.at[j - 1], got2.at[j - 1], send2.at[j - 1], recv2.at[j - 1], second_peer(j))
-
-    def copyw(j):
-        return remote(
-            dense_mid.at[j - 1], dense_got.at[j - 1], wsend.at[j - 1], wrecv.at[j - 1], second_peer(j)
+        def copy(k):
+            src, dst, who = pairs[k]
+            return remote(src, dst, send.at[k], recv.at[k], who)
+
+        return copy
+
+    half = rows // 2
+
+    def ring1(j):
+        return ring(
+            lambda d: parts.at[shard_of(core, y, x, d, j)],
+            half,
+            rows,
+            (via_plus.at[j], via_minus.at[j]),
+            (acc_plus.at[j], acc_minus.at[j]),
+            (got_plus.at[j], got_minus.at[j]),
+            send1.at[j],
+            recv1.at[j],
+            first_peer(1),
+            first_peer(3),
         )
+
+    def ring2():
+        return ring(
+            lambda d: mid.at[d],
+            half,
+            rows,
+            (via2.at[0], via2.at[1]),
+            (mid.at[1, pl.ds(0, half)], mid.at[3, pl.ds(half, half)]),
+            (got2.at[0], got2.at[1]),
+            send2,
+            recv2,
+            second_peer(1),
+            second_peer(3),
+        )
+
+    cut = 80
+
+    def ringw():
+        return ring(
+            lambda d: dense_mid.at[d],
+            cut,
+            PIECE,
+            (dense_via_plus, dense_via_minus),
+            (dense_mid.at[1, pl.ds(0, cut)], dense_mid.at[3, pl.ds(cut, PIECE - cut)]),
+            (dense_got.at[0], dense_got.at[1]),
+            wsend,
+            wrecv,
+            second_peer(1),
+            second_peer(3),
+        )
+
+    def go(copies, *which):
+        for k in which:
+            copies(k).start()
+
+    def arrived(copies, *which):
+        for k in which:
+            copies(k).wait_recv()
 
     def copyz(d):
         return remote(
@@ -358,46 +420,92 @@
     def local_dense(d):
         return pltpu.make_async_copy((s0, s1, s2, s3)[d], dense.at[d], local_sem.at[d])
 
-    def local_own(j):
-        return pltpu.make_async_copy(
-            parts.at[shard_of(core, y, x, 0, j)], own.at[j], local_sem.at[4 + j]
-        )
-
+    def forward(j):
+        to_plus, to_minus = shard_of(core, y, x, 1, j), shard_of(core, y, x, 3, j)
+        copies = ring1(j)
+        arrived(copies, 0, 1)
+
+        def block(i, c):
+            at = pl.ds(pl.multiple_of(i * 128, 128), 128)
+            later = pl.ds(pl.multiple_of(half + i * 128, 128), 128)
+            acc_plus[j, at, :] = (
+                parts[to_plus, at, :].astype(f32) + via_plus[j, at, :].astype(f32)
+            ).astype(bf16)
+            acc_minus[j, at, :] = (
+                parts[to_minus, later, :].astype(f32) + via_minus[j, at, :].astype(f32)
+            ).astype(bf16)
+            return c
+
+        lax.fori_loop(0, half // 128, block, 0)
+        go(copies, 4, 5)
+
+    def row_mid(j):
+        arrived(ring1(j), 2, 3, 4, 5)
+        mine = shard_of(core, y, x, 0, j)
+
+        def block(i, c):
+            at = pl.ds(pl.multiple_of(i * 128, 128), 128)
+            total = parts[mine, at, :].astype(f32)
+            total = total + got_plus[j, at, :].astype(f32) + got_minus[j, at, :].astype(f32)
+            mid[j, at, :] = total.astype(bf16)
+            return c
+
+        lax.fori_loop(0, rows // 128, block, 0)
+
+    go(ring1(2), 0, 1)
     for d in range(4):
         local_dense(d).start()
-    for j in (1, 2, 3, 0):
-        for d in (1, 2, 3):
-            copy1(d, j).start()
-    for j in range(4):
-        local_own(j).start()
+    go(ring1(2), 2, 3)
+    go(ring1(1), 0, 1)
     for d in range(4):
         local_dense(d).wait()
 
-    def dense_sum(j, at):
-        total = dense[0, j, at, :].astype(f32)
-        for d in (1, 2, 3):
-            total = total + dense[d, j, at, :].astype(f32)
-        return total
-
-    for j in (1, 2, 3):
+    for j in (2, 1, 3, 0):
 
         def dense_block(i, c):
             at = pl.ds(pl.multiple_of(i * 16, 16), 16)
-            dense_mid[j - 1, at, :] = dense_sum(j, at).astype(bf16)
+            total = dense[0, j, at, :].astype(f32)
+            for d in (1, 2, 3):
+                total = total + dense[d, j, at, :].astype(f32)
+            dense_mid[j, at, :] = total.astype(bf16)
             return c
 
         lax.fori_loop(0, PIECE // 16, dense_block, 0)
-        copyw(j).start()
-    for j in range(4):
-        local_own(j).wait()
-    for j in (1, 2, 3):
-        copyw(j).wait_recv()
+        if j == 2:
+            go(ringw(), 0, 1)
+            forward(2)
+            go(ring1(1), 2, 3)
+            go(ring1(3), 0, 1)
+        elif j != 0:
+            go(ringw(), 2 if j == 1 else 3)
+    arrived(ringw(), 0, 1)
+    for target, came, start, count in (
+        (1, dense_via_plus, 0, cut),
+        (3, dense_via_minus, cut, PIECE - cut),
+    ):
+
+        def dense_add(i, c):
+            at = pl.ds(pl.multiple_of(i * 16, 16), 16)
+            to = pl.ds(pl.multiple_of(start + i * 16, 16), 16)
+            dense_mid[target, to, :] = (
+                dense_mid[target, to, :].astype(f32) + came[at, :].astype(f32)
+            ).astype(bf16)
+            return c
+
+        lax.fori_loop(0, count // 16, dense_add, 0)
+    go(ringw(), 4, 5)
+    forward(1)
+    go(ring1(3), 2, 3)
+    go(ring1(0), 0, 1)
+    forward(3)
+    go(ring1(0), 2, 3)
+
+    arrived(ringw(), 2, 3, 4, 5)
 
     def dense_last(i, c):
         at = pl.ds(pl.multiple_of(i * 16, 16), 16)
-        total = dense_sum(0, at)
-        for j in (1, 2, 3):
-            total = total + dense_got[j - 1, at, :].astype(f32)
+        total = dense_mid[0, at, :].astype(f32)
+        total = total + dense_got[0, at, :].astype(f32) + dense_got[1, at, :].astype(f32)
         total = total.astype(bf16)
         for k in range(Z):
             zparts[k, at, :] = total[:, 128 * k : 128 * k + 128]
@@ -407,25 +515,9 @@
     for d in range(1, Z):
         copyz(d).start()
 
-    def row_sum(j, at):
-        total = own[j, at, :].astype(f32)
-        for d in (1, 2, 3):
-            total = total + got1[d - 1, j, at, :].astype(f32)
-        return total
-
-    def row_mid(j):
-        for d in (1, 2, 3):
-            copy1(d, j).wait_recv()
-
-        def block(i, c):
-            at = pl.ds(pl.multiple_of(i * 128, 128), 128)
-            mid[j - 1, at, :] = row_sum(j, at).astype(bf16)
-            return c
-
-        lax.fori_loop(0, 8, block, 0)
-        copy2(j).start()
-
-    row_mid(1)
+    row_mid(2)
+    go(ring2(), 0, 1)
+    forward(0)
     for d in range(1, Z):
         copyz(d).wait_recv()
     total = zparts[z].astype(f32)
@@ -434,13 +526,25 @@
     final[core, z] = total.astype(bf16)
     for d in range(1, Z):
         copyg(d, z).start()
-    row_mid(2)
+    row_mid(1)
+    go(ring2(), 2)
+    row_mid(3)
+    go(ring2(), 3)
+    arrived(ring2(), 0, 1)
+
+    def mid_add(i, c):
+        at = pl.ds(pl.multiple_of(i * 128, 128), 128)
+        later = pl.ds(pl.multiple_of(half + i * 128, 128), 128)
+        mid[1, at, :] = (mid[1, at, :].astype(f32) + via2[0, at, :].astype(f32)).astype(bf16)
+        mid[3, later, :] = (mid[3, later, :].astype(f32) + via2[1, at, :].astype(f32)).astype(bf16)
+        return c
+
+    lax.fori_loop(0, half // 128, mid_add, 0)
+    go(ring2(), 4, 5)
     for d in range(1, Z):
         copyg(d, lax.rem(z - d + Z, Z)).wait_recv()
     copyc(core).start()
-    row_mid(3)
-    for d in (1, 2, 3):
-        copy1(d, 0).wait_recv()
+    arrived(ring1(0), 2, 3, 4, 5)
     copyc(1 - core).wait_recv()
     for k in range(Z):
         at = slice(128 * k, 128 * k + 128)
@@ -455,25 +559,25 @@
         down_out[48:96, at] = final[1, 2 + k, 96:144, :].astype(f32)
         down_out[96:136, at] = final[1, 4 + k, 96:144, :].astype(f32)[0:40]
         vec_out[:, at] = final[1, 6 + k, 112:128, :].astype(f32)[0:8]
-    for j in (1, 2, 3):
-        copy2(j).wait_recv()
+    arrived(ring2(), 2, 3, 4, 5)
+
+    own = shard_of(core, y, x, 0, 0)
 
     def row_last(i, c):
         at = pl.ds(pl.multiple_of(i * 128, 128), 128)
-        total = row_sum(0, at)
-        for j in (1, 2, 3):
-            total = total + got2[j - 1, at, :].astype(f32)
-        row_out[at, :] = total
-        return c
-
-    lax.fori_loop(0, 8, row_last, 0)
-
-    for d in (1, 2, 3):
-        for j in range(4):
-            copy1(d, j).wait_send()
-    for j in (1, 2, 3):
-        copy2(j).wait_send()
-        copyw(j).wait_send()
+        total = parts[own, at, :].astype(f32)
+        total = total + got_plus[0, at, :].astype(f32) + got_minus[0, at, :].astype(f32)
+        row_out[at, :] = total + got2[0, at, :].astype(f32) + got2[1, at, :].astype(f32)
+        return c
+
+    lax.fori_loop(0, rows // 128, row_last, 0)
+
+    for j in range(4):
+        for k in range(6):
+            ring1(j)(k).wait_send()
+    for k in range(6):
+        ring2()(k).wait_send()
+        ringw()(k).wait_send()
     for d in range(1, Z):
         copyz(d).wait_send()
         copyg(d, z).wait_send()
@@ -484,6 +588,7 @@
     vmem = pl.BlockSpec(memory_space=pltpu.VMEM)
     anywhere = pl.BlockSpec(memory_space=pl.ANY)
     rows, width = parts.shape[1:]
+    half = rows // 2
     dma = pltpu.SemaphoreType.DMA
     return pl.pallas_call(
         exchange_kernel,
@@ -495,26 +600,33 @@
             jax.ShapeDtypeStruct((136, 256), f32),
             jax.ShapeDtypeStruct((8, 256), f32),
         ),
-        in_specs=[anywhere] * 5,
+        in_specs=[vmem] + [anywhere] * 4,
         out_specs=(vmem,) * 6,
         scratch_shapes=[
+            pltpu.VMEM((4, half, width), bf16),
+            pltpu.VMEM((4, half, width), bf16),
+            pltpu.VMEM((4, half, width), bf16),
+            pltpu.VMEM((4, half, width), bf16),
             pltpu.VMEM((4, rows, width), bf16),
-            pltpu.VMEM((3, 4, rows, width), bf16),
-            pltpu.VMEM((3, rows, width), bf16),
-            pltpu.VMEM((3, rows, width), bf16),
+            pltpu.VMEM((4, rows, width), bf16),
+            pltpu.VMEM((4, rows, width), bf16),
+            pltpu.VMEM((2, half, width), bf16),
+            pltpu.VMEM((2, rows, width), bf16),
             pltpu.VMEM((4, 4, PIECE, WIDE), bf16),
-            pltpu.VMEM((3, PIECE, WIDE), bf16),
-            pltpu.VMEM((3, PIECE, WIDE), bf16),
+            pltpu.VMEM((4, PIECE, WIDE), bf16),
+            pltpu.VMEM((80, WIDE), bf16),
+            pltpu.VMEM((64, WIDE), bf16),
+            pltpu.VMEM((2, PIECE, WIDE), bf16),
             pltpu.VMEM((Z, PIECE, 128), bf16),
             pltpu.VMEM((Z - 1, PIECE, 128), bf16),
             pltpu.VMEM((2, Z, PIECE, 128), bf16),
-            dma((8,)),
-            dma((3, 4)),
-            dma((3, 4)),
-            dma((3,)),
-            dma((3,)),
-            dma((3,)),
-            dma((3,)),
+            dma((4,)),
+            dma((4, 6)),
+            dma((4, 6)),
+            dma((6,)),
+            dma((6,)),
+            dma((6,)),
+            dma((6,)),
             dma((Z - 1,)),
             dma((Z - 1,)),
             dma((Z - 1,)),
@@ -523,7 +635,7 @@
             dma,
         ],
         compiler_params=pltpu.CompilerParams(
-            collective_id=1, has_side_effects=True, vmem_limit_bytes=48 << 20
+            collective_id=1, has_side_effects=True, vmem_limit_bytes=44 << 20
         ),
     )(parts, *sums)
 
@@ -541,36 +653,48 @@
     return pairs
 
 
-def scatter_kernel(s_ref, v_ref, o_ref, wide, *accs):
+def scatter_kernel(slots_ref, v_ref, o_ref, s_ref, wide, sem, *accs):
     count = v_ref.shape[0]
     slots, width = o_ref.shape
-    unroll = 16
+    row = lax.axis_index("row")
+    per_table = slots_ref.shape[1] // (2 * Z)
+    own = per_table // (Y * X)
+
+    def fetch(t):
+        at = (t // 2) * per_table + row * own + (t % 2) * 128
+        return pltpu.make_async_copy(
+            slots_ref.at[:, pl.ds(pl.multiple_of(at, 128), 128)], s_ref.at[t], sem.at[t]
+        )
+
+    for t in range(count // 128):
+        fetch(t).start()
 
     def clear(i, c):
         for acc in accs:
-            acc[pl.ds(pl.multiple_of(i * 256, 256), 256), :] = jnp.zeros((256, width), jnp.float32)
+            acc[pl.ds(pl.multiple_of(i * 256, 256), 256), :] = jnp.zeros((256, width), f32)
         return c
 
     lax.fori_loop(0, slots // 256, clear, 0)
-    wide[...] = v_ref[...].astype(jnp.float32)
+    wide[...] = v_ref[...].astype(f32)
+    for t in range(count // 128):
+        fetch(t).wait()
 
     def step(g, c):
-        base = g * unroll
-        for i in range(0, unroll, 2):
-            row0 = wide[pl.ds(base + i, 1), :]
-            row1 = wide[pl.ds(base + i + 1, 1), :]
+        for i in range(0, 128, 2):
+            row0 = wide[pl.ds(g * 128 + i, 1), :]
+            row1 = wide[pl.ds(g * 128 + i + 1, 1), :]
             for which, acc in enumerate(accs):
-                s0 = s_ref[which * count + base + i]
-                s1 = s_ref[which * count + base + i + 1]
-                old0 = acc[pl.ds(s0, 1), :]
-                old1 = acc[pl.ds(s1, 1), :]
+                slot0 = s_ref[g, which, i]
+                slot1 = s_ref[g, which, i + 1]
+                old0 = acc[pl.ds(slot0, 1), :]
+                old1 = acc[pl.ds(slot1, 1), :]
                 new0 = old0 + row0
-                new1 = jnp.where(s0 == s1, new0, old1) + row1
-                acc[pl.ds(s0, 1), :] = new0
-                acc[pl.ds(s1, 1), :] = new1
-        return c
-
-    lax.fori_loop(0, count // unroll, step, 0)
+                new1 = jnp.where(slot0 == slot1, new0, old1) + row1
+                acc[pl.ds(slot0, 1), :] = new0
+                acc[pl.ds(slot1, 1), :] = new1
+        return c
+
+    lax.fori_loop(0, count // 128, step, 0)
 
     def finish(i, c):
         at = pl.ds(pl.multiple_of(i * 128, 128), 128)
@@ -583,17 +707,21 @@
     lax.fori_loop(0, slots // 128, finish, 0)
 
 
-def scatter_rows(slots, values):
+def scatter_rows(slots, values, total_slots):
     count, width = values.shape
-    total_slots = slots.size
+    hot = slots.shape[0]
     return pl.pallas_call(
         scatter_kernel,
-        out_shape=jax.ShapeDtypeStruct((total_slots, width), jnp.bfloat16),
-        in_specs=[pl.BlockSpec(memory_space=pltpu.SMEM), pl.BlockSpec(memory_space=pltpu.VMEM)],
+        out_shape=jax.ShapeDtypeStruct((total_slots, width), bf16),
+        in_specs=[pl.BlockSpec(memory_space=pl.ANY), pl.BlockSpec(memory_space=pltpu.VMEM)],
         out_specs=pl.BlockSpec(memory_space=pltpu.VMEM),
-        scratch_shapes=[pltpu.VMEM((count, width), jnp.float32)]
-        + [pltpu.VMEM((total_slots, width), jnp.float32)] * (slots.size // count),
-        compiler_params=pltpu.CompilerParams(vmem_limit_bytes=58 << 20),
+        scratch_shapes=[
+            pltpu.SMEM((count // 128, hot, 128), jnp.int32),
+            pltpu.VMEM((count, width), f32),
+            pltpu.SemaphoreType.DMA((count // 128,)),
+        ]
+        + [pltpu.VMEM((total_slots, width), f32)] * hot,
+        compiler_params=pltpu.CompilerParams(vmem_limit_bytes=44 << 20),
         cost_estimate=pl.CostEstimate(
             flops=10_000_000, bytes_accessed=100_000_000, transcendentals=0
         ),
@@ -631,20 +759,19 @@
     width = dense_feat.shape[1]
     n_table = lax.axis_size("table")
     n_row = lax.axis_size("row")
-    hot_count = lookup_slots.shape[2]
     samples = n_table * batch_dev
-    row_pos = lax.axis_index("row")
+    u_shard = 1024
     pooled_grad = delta_stacked[:, width:].astype(jnp.bfloat16).reshape(batch_dev, n_table, width)
     saved, pooled_grad = lax.optimization_barrier((saved, pooled_grad))
     received = lax.all_to_all(pooled_grad, "table", split_axis=1, concat_axis=0, tiled=True)
-    mine = jnp.transpose(lookup_slots[0]).reshape(hot_count, n_table, n_row, batch_dev)
-    mine = lax.dynamic_index_in_dim(mine, row_pos, axis=2, keepdims=False)
     kept, *away = weight_grads(saved)
     came = [
         lax.ppermute(part, ("table", "row"), first_axis_pairs(shift + 1))
         for shift, part in enumerate(away)
     ]
-    partial = scatter_rows(mine.reshape(-1), received.reshape(samples, width))
+    partial = scatter_rows(
+        jnp.transpose(lookup_slots[0]), received.reshape(samples, width), n_row * u_shard
+    )
     row_grads, g_h1, g_h2, g_up, g_down, vecs = exchange(
         partial.reshape(n_row, -1, width), [kept] + came
     )

time: 146 us -> 135 us (0.925)
  the two profiles are of different devices: /device:TPU:2 before, /device:TPU:1 now
where the time goes in v3:
time: 135 us
  Pallas kernels  89.5 us (66%)
  local copies, waits for them, and re-layouts  21.5 us (16%)
  starting transfers between devices  15 us (11%)
  matrix products  6.89 us (5%)
    pallas_call x1, Pallas kernels, exchange(): pl.pallas_call(exchange_kernel, out_shape=(jax.ShapeDtypeStruct((rows, wi...  45.3 us
    pallas_call x1, Pallas kernels, scatter_rows(): pl.pallas_call(scatter_kernel, out_shape=jax.ShapeDtypeStruct((total_slot...  26 us
    pallas_call x1, Pallas kernels, weight_grads(): pl.pallas_call(weight_kernel, out_shape=(piece,) * 4, in_specs=[vmem] * 9...  18.2 us
    unnamed x51, local copies, waits for them, and re-layouts  17.8 us
    all_to_all x1, starting transfers between devices, local(): lax.all_to_all(pooled_grad, 'table', split_axis=1, concat_axis=0, tiled=T...  9.98 us
    ppermute x3, starting transfers between devices, local(): lax.ppermute(part, ('table', 'row'), first_axis_pairs(shift + 1))  5.05 us
  transfers between devices with their start and end apart: 4, of which 0 were waited for; matrix products, arithmetic and copies ran while one was open for 0% of the time, Pallas kernels for 33%

profile of v3, /device:TPU:1, one launch (start us, length us, event | category | flops | bytes accessed | tf_op | source)
XLA Modules:
  0.0 134.7 jit_solution(14722780555209645332)
XLA Ops:
  0.7 1.0 constant_dynamic-update-slice_fusion.1
  1.7 1.3 constant_dynamic-update-slice_fusion.stacked
  4.8 2.1 %copy-done.15 = bf16[2176,1024]{1,0:T(8,128)(2,1)S(1)} copy-done((bf16[2176,1024]{1,0:T(8,128)(2,1)S(1)}, bf16[2176,1024]{1,0:T(8,128)(2,1)}, u32[]{:S(2)}) %copy-start.15) | copy-done | bytes 4456472
  6.9 1.6 %multiply_convert_fusion.2 = (bf16[256,1024]{1,0:T(8,128)(2,1)S(1)}, f32[256,1024]{1,0:T(8,128)S(1)}) fusion(f32[1024]{0:T(1024)S(1)} %copy-done.20, bf16[256,2176]{1,0:T(8,128)(2,1)S(1)} %get-tuple-element.31.crossed, bf16[2176,1024]{1,0:T(8,128)(2,1)S(1)} %copy-done.15), kind=kOutput, calls=%fused_computation.23 | convolution fusion | flops 1142423552 | bytes 7147520 | tf_op jit(solution)/shard_map/dot_general | solution.py:34
  8.6 1.0 fusion.4
  10.1 0.9 fusion.3.delta_first
  11.8 1.4 %fusion = (bf16[256,2176]{1,0:T(8,128)(2,1)S(1)}, f32[256,2176]{1,0:T(8,128)S(1)}) fusion(bf16[256,2176]{1,0:T(8,128)(2,1)S(1)} %constant_dynamic-update-slice_fusion.stacked, bf16[256,1024]{1,0:T(8,128)(2,1)S(1)} %fusion.3.delta_first, bf16[2176,1024]{1,0:T(8,128)(2,1)S(1)} %copy-done.15), kind=kOutput, calls=%fused_computation.3 | convolution fusion | flops 1142521856 | bytes 9437184 | tf_op jit(solution)/shard_map/dot_general | solution.py:47
  15.3 1.3 copy.22
  16.6 10.0 %all-to-all-start = ((bf16[256,16,128]{2,0,1:T(8,128)(2,1)}), bf16[256,16,128]{2,0,1:T(8,128)(2,1)}, u32[]{:S(2)}, u32[]{:S(2)}) async-start(bf16[256,16,128]{2,0,1:T(8,128)(2,1)} %copy.22), calls=%async_computation | async-start | bytes 2097152 | tf_op jit(solution)/shard_map/all_to_all | solution.py:766
  26.6 1.2 copy-done.3
  27.8 1.2 copy-done.6
  29.1 1.0 copy-done.9
  30.1 1.0 copy-done.11
  31.2 1.0 copy-done.13
  32.2 18.2 %shard_map.188 = (bf16[4,144,1024]{2,1,0:T(8,128)(2,1)}, bf16[4,144,1024]{2,1,0:T(8,128)(2,1)}, bf16[4,144,1024]{2,1,0:T(8,128)(2,1)}, bf16[4,144,1024]{2,1,0:T(8,128)(2,1)}) custom-call(bf16[256,2176]{1,0:T(8,128)(2,1)S(1)} %constant_dynamic-update-slice_fusion.stacked, bf16[256,2176]{1,0:T(8,128)(2,1)S(1)} %copy-done.6, ...), custom_call_target="tpu_custom_call" | custom-call | flops 2300000000 | bytes 60000000 | tf_op jit(solution)/shard_map/pallas_call | solution.py:247
  50.4 1.4 %collective-permute-start = (bf16[4,144,1024]{2,1,0:T(8,128)(2,1)}, bf16[4,144,1024]{2,1,0:T(8,128)(2,1)S(1)}, u32[]{:S(2)}, u32[]{:S(2)}) collective-permute-start(bf16[4,144,1024]{2,1,0:T(8,128)(2,1)} %get-tuple-element.40), channel_id=1, source_target_pairs={{0,1},{1,2},{2,3},{3,0},{4,5},{5,6},{6,7},{7,4},{8,9},{9,10},{10,1... | collective-permute-start | bytes 3538952 | tf_op jit(solution)/shard_map/ppermute | solution.py:769
  51.8 2.6 %collective-permute-start.1 = (bf16[4,144,1024]{2,1,0:T(8,128)(2,1)}, bf16[4,144,1024]{2,1,0:T(8,128)(2,1)}, u32[]{:S(2)}, u32[]{:S(2)}) collective-permute-start(bf16[4,144,1024]{2,1,0:T(8,128)(2,1)} %get-tuple-element.41), channel_id=1, source_target_pairs={{0,2},{1,3},{2,0},{3,1},{4,6},{5,7},{6,4},{7,5},{8,10},{9,11},{10,... | collective-permute-start | bytes 3538952 | tf_op jit(solution)/shard_map/ppermute | solution.py:769
  54.4 1.1 collective-permute-start.2
  55.5 1.2 copy-done.7
  56.7 26.0 %shard_map.187 = bf16[16384,128]{1,0:T(8,128)(2,1)S(1)} custom-call(s32[4,65536]{1,0:T(4,128)S(1)} %bitcast.38, bf16[4096,128]{1,0:T(8,128)(2,1)} %bitcast.5.v_ref), custom_call_target="tpu_custom_call" | custom-call | flops 10000000 | bytes 100000000 | tf_op jit(solution)/shard_map/pallas_call | solution.py:713
  82.7 1.9 %copy-done.1 = bf16[16384,128]{1,0:T(8,128)(2,1)} copy-done((bf16[16384,128]{1,0:T(8,128)(2,1)}, bf16[16384,128]{1,0:T(8,128)(2,1)S(1)}, u32[]{:S(2)}) %copy-start.1) | copy-done | bytes 4194328
  84.7 45.3 %shard_map.189 = (f32[1024,128]{1,0:T(8,128)S(1)}, f32[136,1024]{1,0:T(8,128)S(1)}, f32[64,1024]{1,0:T(8,128)S(1)}, f32[16,2176]{1,0:T(8,128)S(1)}, f32[136,256]{1,0:T(8,128)S(1)}, /*index=5*/f32[8,256]{1,0:T(8,128)S(1)}) custom-call(bf16[16,1024,128]{2,1,0:T(8,128)(2,1)} %bitcast.37, bf16[4,144,1024]{2,1,0:T(8,128)(2,1)S(1)} %copy-done.4, ...), custom_call_target="tpu_custom_call" | custom-call | tf_op jit(solution)/shard_map/pallas_call | solution.py:593
  131.0 0.8 copy.30
  133.1 0.8 copy.33
  (53 shorter events, 8.3 us)
Async XLA Ops:
  0.6 7.9 %copy-start = (bf16[1024,1024]{1,0:T(8,128)(2,1)S(1)}, bf16[1024,1024]{1,0:T(8,128)(2,1)}, u32[]{:S(2)}) copy-start(bf16[1024,1024]{1,0:T(8,128)(2,1)} %param.20) | copy-start | bytes 6291460
  0.7 2.3 %copy-start.16 = (bf16[2176,256]{1,0:T(8,128)(2,1)S(1)}, bf16[2176,256]{1,0:T(8,128)(2,1)}, u32[]{:S(2)}) copy-start(bf16[2176,256]{1,0:T(8,128)(2,1)} %param.15) | copy-start | bytes 3342340
  3.0 1.3 copy-start.14
  3.0 1.2 copy-start.17
  4.3 2.7 %copy-start.15 = (bf16[2176,1024]{1,0:T(8,128)(2,1)S(1)}, bf16[2176,1024]{1,0:T(8,128)(2,1)}, u32[]{:S(2)}) copy-start(bf16[2176,1024]{1,0:T(8,128)(2,1)} %param.18) | copy-start | bytes 13369348
  4.3 2.7 %copy-start.20 = (f32[1024]{0:T(1024)S(1)}, f32[1024]{0:T(1024)}, u32[]{:S(2)}) copy-start(f32[1024]{0:T(1024)} %param.19) | copy-start | bytes 12292
  4.8 3.7 %copy-start.5 = (bf16[256,2176]{1,0:T(8,128)(2,1)}, bf16[256,2176]{1,0:T(8,128)(2,1)S(1)}, u32[]{:S(2)}) copy-start(bf16[256,2176]{1,0:T(8,128)(2,1)S(1)} %get-tuple-element.31.crossed) | copy-start | bytes 3342340
  6.9 1.6 %copy-start.18 = (f32[1024]{0:T(1024)S(1)}, f32[1024]{0:T(1024)}, u32[]{:S(2)}) copy-start(f32[1024]{0:T(1024)} %param.22) | copy-start | bytes 12292
  6.9 1.6 %copy-start.21 = (f32[1024]{0:T(1024)S(1)}, f32[1024]{0:T(1024)}, u32[]{:S(2)}) copy-start(f32[1024]{0:T(1024)} %param.21) | copy-start | bytes 12292
  8.5 1.1 copy-start.12
  8.5 1.0 copy-start.19
  11.8 1.4 %copy-start.8 = (bf16[256,1024]{1,0:T(8,128)(2,1)}, bf16[256,1024]{1,0:T(8,128)(2,1)S(1)}, u32[]{:S(2)}) copy-start(bf16[256,1024]{1,0:T(8,128)(2,1)S(1)} %fusion.3.delta_first) | copy-start | bytes 1572868
  16.6 38.9 %all-to-all-start = ((bf16[256,16,128]{2,0,1:T(8,128)(2,1)}), bf16[256,16,128]{2,0,1:T(8,128)(2,1)}, u32[]{:S(2)}, u32[]{:S(2)}) async-start(bf16[256,16,128]{2,0,1:T(8,128)(2,1)} %copy.22), calls=%async_computation | async-start | bytes 2097152 | tf_op jit(solution)/shard_map/all_to_all | solution.py:766
  26.6 1.2 copy-start.3
  27.8 1.2 copy-start.6
  29.1 1.0 copy-start.9
  30.1 1.0 copy-start.11
  31.2 1.0 copy-start.13
  50.4 34.2 %collective-permute-start = (bf16[4,144,1024]{2,1,0:T(8,128)(2,1)}, bf16[4,144,1024]{2,1,0:T(8,128)(2,1)S(1)}, u32[]{:S(2)}, u32[]{:S(2)}) collective-permute-start(bf16[4,144,1024]{2,1,0:T(8,128)(2,1)} %get-tuple-element.40), channel_id=1, source_target_pairs={{0,1},{1,2},{2,3},{3,0},{4,5},{5,6},{6,7},{7,4},{8,9},{9,10},{10,1... | collective-permute-start | bytes 3538952 | tf_op jit(solution)/shard_map/ppermute | solution.py:769
  51.8 32.9 %collective-permute-start.1 = (bf16[4,144,1024]{2,1,0:T(8,128)(2,1)}, bf16[4,144,1024]{2,1,0:T(8,128)(2,1)}, u32[]{:S(2)}, u32[]{:S(2)}) collective-permute-start(bf16[4,144,1024]{2,1,0:T(8,128)(2,1)} %get-tuple-element.41), channel_id=1, source_target_pairs={{0,2},{1,3},{2,0},{3,1},{4,6},{5,7},{6,4},{7,5},{8,10},{9,11},{10,... | collective-permute-start | bytes 3538952 | tf_op jit(solution)/shard_map/ppermute | solution.py:769
  54.4 30.2 %collective-permute-start.2 = (bf16[4,144,1024]{2,1,0:T(8,128)(2,1)}, bf16[4,144,1024]{2,1,0:T(8,128)(2,1)}, u32[]{:S(2)}, u32[]{:S(2)}) collective-permute-start(bf16[4,144,1024]{2,1,0:T(8,128)(2,1)} %get-tuple-element.42), channel_id=1, source_target_pairs={{0,3},{1,0},{2,1},{3,2},{4,7},{5,4},{6,5},{7,6},{8,11},{9,8},{10,9... | collective-permute-start | bytes 3538952 | tf_op jit(solution)/shard_map/ppermute | solution.py:769
  55.5 1.2 copy-start.7
  56.7 27.9 %copy-start.4 = (bf16[4,144,1024]{2,1,0:T(8,128)(2,1)S(1)}, bf16[4,144,1024]{2,1,0:T(8,128)(2,1)}, u32[]{:S(2)}) copy-start(bf16[4,144,1024]{2,1,0:T(8,128)(2,1)} %get-tuple-element.39.s0) | copy-start | bytes 3538948
  82.7 2.0 %copy-start.1 = (bf16[16384,128]{1,0:T(8,128)(2,1)}, bf16[16384,128]{1,0:T(8,128)(2,1)S(1)}, u32[]{:S(2)}) copy-start(bf16[16384,128]{1,0:T(8,128)(2,1)S(1)} %shard_map.187) | copy-start | bytes 12582916
  (2 other events, 1.8 us)

commit v4 on v3

v4 whole, which is shorter than its diff:
```python
import jax
import jax.numpy as jnp
from jax import lax
from jax.experimental import pallas as pl
from jax.experimental.pallas import tpu as pltpu
from jax.sharding import PartitionSpec as P

loss_scale = 16.0


MESH = pl.DeviceIdType.MESH
X, Y, Z = 4, 4, 8
PIECE = 144
WIDE = 1024
f32, bf16 = jnp.float32, jnp.bfloat16


def place():
    table = lax.axis_index("table")
    row = lax.axis_index("row")
    core, z = lax.rem(table, 2), table // 2
    y, x = row // X, lax.rem(row, X)
    return table, row, core, z, y, x


def slot_of(half, shard, y, x):
    dy = lax.rem(shard // X - y + Y, Y)
    dx = lax.rem(lax.rem(shard, X) - x + X, X)
    return dx * 4 + dy if half == 0 else dy * 4 + dx


def shard_of(core, y, x, first, second):
    dx = first * (1 - core) + second * core
    dy = second * (1 - core) + first * core
    return lax.rem(y + dy, Y) * X + lax.rem(x + dx, X)


def transposed(dst, src):
    for i in range(src.shape[1] // 128):
        at = slice(128 * i, 128 * i + 128)
        dst[at, :] = src[:, at].T


def ring(chunk, cut, size, vias, accs, gots, send, recv, plus, minus):
    low, high = pl.ds(0, cut), pl.ds(cut, size - cut)
    pairs = (
        (lambda: chunk(2).at[low], vias[0], plus),
        (lambda: chunk(2).at[high], vias[1], minus),
        (lambda: chunk(1).at[high], gots[0].at[high], plus),
        (lambda: chunk(3).at[low], gots[1].at[low], minus),
        (lambda: accs[0], gots[0].at[low], plus),
        (lambda: accs[1], gots[1].at[high], minus),
    )

    def copy(k):
        src, dst, who = pairs[k]
        return remote(src(), dst, send.at[k], recv.at[k], who)

    return copy


def remote(src, dst, s, r, who):
    return pltpu.make_async_remote_copy(
        src_ref=src, dst_ref=dst, send_sem=s, recv_sem=r, device_id=who, device_id_type=MESH
    )


def go(copies, *which):
    for k in which:
        copies(k).start()


def arrived(copies, *which):
    for k in which:
        copies(k).wait_recv()


def dot(a, b):
    return jnp.dot(a, b, preferred_element_type=f32)


def dot_t(a, b):
    return lax.dot_general(a, b, (((1,), (1,)), ((), ())), preferred_element_type=f32)


def tiles(body, width):
    for i in range(width // 256):
        body(slice(256 * i, 256 * i + 256), i)
    if width % 256:
        body(slice(width - width % 256, width), width // 256)


def dense_kernel(
    dense_feat,
    pooled,
    cross_down,
    cross_up,
    w_hidden1,
    w_hidden2,
    labels,
    cross_bias,
    bias1,
    bias2,
    w_logit,
    received,
    out,
    stacked,
    down_w,
    up_w,
    w1,
    w2,
    wide_plus,
    crossed,
    slope1,
    slope2,
    act_first,
    act_second,
    delta_second,
    delta_first,
    delta_crossed,
    delta_widened,
    reduced,
    delta_reduced,
    grad_logit,
    ready,
    packed,
    landed,
    flipped,
    small,
    via_plus,
    via_minus,
    got_plus,
    got_minus,
    load_sem,
    tsend,
    trecv,
    send_sem,
    recv_sem,
    send1,
    recv1,
    own_sem,
):
    table, row, core, z, y, x = place()
    n_table = 2 * Z
    other = z * 2 + 1 - core

    loads = [
        pltpu.make_async_copy(dense_feat, stacked.at[:, pl.ds(0, 128)], load_sem.at[0]),
        pltpu.make_async_copy(pooled, stacked.at[:, pl.ds(128, 2048)], load_sem.at[1]),
        pltpu.make_async_copy(cross_down, down_w, load_sem.at[2]),
        pltpu.make_async_copy(cross_up, up_w, load_sem.at[3]),
    ]
    for k in range(4):
        part = pl.ds(544 * k, 544)
        loads.append(pltpu.make_async_copy(w_hidden1.at[part], w1.at[part], load_sem.at[4 + k]))
    for k in range(2):
        part = pl.ds(512 * k, 512)
        loads.append(pltpu.make_async_copy(w_hidden2.at[part], w2.at[part], load_sem.at[8 + k]))
    for one in loads:
        one.start()

    def first_peer(d):
        return (table, shard_of(core, y, x, d, 0))

    barrier = pltpu.get_barrier_semaphore()
    for d in range(1, n_table):
        who = (lax.rem(table + d, n_table), row)
        pl.semaphore_signal(barrier, inc=1, device_id=who, device_id_type=MESH)
    for d in (1, 3):
        pl.semaphore_signal(barrier, inc=1, device_id=first_peer(d), device_id_type=MESH)

    def exchange_table(d):
        to = lax.rem(table + d, n_table)
        return remote(
            ready.at[to + 1], received.at[table], tsend.at[d - 1], trecv.at[d - 1], (to, row)
        )

    def came_table(d):
        came = lax.rem(table - d + n_table, n_table)
        return remote(
            ready.at[came + 1], received.at[came], tsend.at[d - 1], trecv.at[d - 1], (came, row)
        )

    def own_table():
        return pltpu.make_async_copy(ready.at[table + 1], received.at[table], own_sem)

    for k in (0, 1, 2):
        loads[k].wait()
    reduced[...] = dot(stacked[...], down_w[...]).astype(bf16)
    loads[3].wait()

    def cross(at, i):
        widened = dot(reduced[...], up_w[:, at]) + cross_bias[:, at]
        base = stacked[:, at].astype(f32)
        crossed[:, at] = (base * widened + base).astype(bf16)
        wide_plus[:, at] = widened + 1.0

    tiles(cross, 2176)
    for k in range(4, 8):
        loads[k].wait()

    def first_layer(at, i):
        pre = dot(crossed[...], w1[:, at]) + bias1[:, at]
        sig = jax.nn.sigmoid(pre)
        act_first[:, at] = (pre * sig).astype(bf16)
        slope1[:, at] = sig * (1.0 + pre * (1.0 - sig))

    tiles(first_layer, 1024)
    for k in range(8, 10):
        loads[k].wait()

    def second_layer(at, logits):
        pre = dot(act_first[...], w2[:, at]) + bias2[:, at]
        sig = jax.nn.sigmoid(pre)
        act = (pre * sig).astype(bf16)
        act_second[:, at] = act
        slope2[:, at] = sig * (1.0 + pre * (1.0 - sig))
        return logits + jnp.sum(act.astype(f32) * w_logit[:, at], axis=1, keepdims=True)

    logits = jnp.zeros((256, 1), f32)
    for i in range(1024 // 256):
        logits = second_layer(slice(256 * i, 256 * i + 256), logits)
    same = lax.broadcasted_iota(jnp.int32, (256, 256), 0) == lax.broadcasted_iota(
        jnp.int32, (256, 256), 1
    )
    label = jnp.sum(jnp.where(same, labels[...].astype(f32), 0.0), axis=1, keepdims=True)
    delta_logit = loss_scale * (jax.nn.sigmoid(logits) - label)

    def back_second(at, i):
        delta_second[:, at] = (delta_logit * w_logit[:, at] * slope2[:, at]).astype(bf16)
        grad_logit[:, at] = jnp.sum(
            act_second[:, at].astype(f32) * delta_logit, axis=0, keepdims=True
        )

    tiles(back_second, 1024)

    def back_first(at, i):
        back = dot_t(delta_second[...], w2[at, :])
        delta_first[:, at] = (back * slope1[:, at]).astype(bf16)

    tiles(back_first, 1024)

    def back_cross(at, i):
        delta = dot_t(delta_first[...], w1[at, :])
        delta_crossed[:, at] = delta
        delta_widened[:, at] = (delta * stacked[:, at].astype(f32)).astype(bf16)

    tiles(back_cross, 2176)
    delta_reduced[...] = dot_t(delta_widened[...], up_w[...]).astype(bf16)

    def back_stacked(at, i):
        delta = delta_crossed[:, at] * wide_plus[:, at] + dot_t(delta_reduced[...], down_w[at, :])
        for k in range(delta.shape[1] // 128):
            ready[2 * i + k] = delta[:, 128 * k : 128 * k + 128].astype(bf16)

    tiles(back_stacked, 2176)
    pl.semaphore_wait(barrier, n_table + 1)
    for d in range(1, n_table):
        exchange_table(d).start()
    own_table().start()

    def copy(half, slot):
        return remote(
            packed.at[half, slot], landed.at[slot], send_sem.at[slot], recv_sem.at[slot], (other, row)
        )

    transposed(flipped, act_first)

    def second(i, c):
        m = dot(flipped[slice(256 * i, 256 * i + 256), :], delta_second[...])
        for k in range(4):
            packed[1, slot_of(1, i * 4 + k, y, x), 0:64, :] = m[64 * k : 64 * k + 64].astype(bf16)
        return c

    for i in range(4):
        second(i, 0)

    transposed(small, reduced)

    def up(i, c):
        left = small[slice(64 * i, 64 * i + 64), :]
        m0 = dot(left, delta_widened[:, 0:1024])
        m1 = dot(left, delta_widened[:, 1024:2048])
        m2 = dot(left, delta_widened[:, 2048:2176])
        for k in range(4):
            slot = slot_of(1, i * 4 + k, y, x)
            part = slice(16 * k, 16 * k + 16)
            packed[1, slot, 64:80, :] = m0[part].astype(bf16)
            packed[1, slot, 80:96, :] = m1[part].astype(bf16)
            packed[1, slot, 96:112, 768:896] = m2[part].astype(bf16)
            packed[1, slot, 96:112, 896:1024] = jnp.zeros((16, 128), bf16)
            packed[1, slot, 128:144, 768:1024] = jnp.zeros((16, 256), bf16)
        return c

    for i in range(4):
        up(i, 0)

    transposed(flipped, stacked)

    def down(i, c):
        m = dot(flipped[slice(272 * i, 272 * i + 272), :], delta_reduced[...])
        for k in range(2):
            slot = slot_of(1, i * 2 + k, y, x)
            d = m[136 * k : 136 * k + 136]
            packed[1, slot, 96:144, 0:256] = d[0:48].astype(bf16)
            packed[1, slot, 96:144, 256:512] = d[48:96].astype(bf16)
            last = jnp.concatenate([d[96:136], jnp.zeros((8, 256), f32)], axis=0)
            packed[1, slot, 96:144, 512:768] = last.astype(bf16)
        return c

    for i in range(8):
        down(i, 0)

    ones = jnp.ones((8, 256), bf16)
    wide_sums = dot(ones, delta_widened[...])
    which = lax.broadcasted_iota(jnp.int32, (8, 1024), 0)
    sums = jnp.where(which == 1, dot(ones, delta_first[...]), dot(ones, delta_second[...]))
    sums = jnp.where(which == 3, grad_logit[...], sums)
    first_row = which[:, 0:256] == 0
    for shard in range(16):
        a = wide_sums if shard == 0 else pltpu.roll(wide_sums, 2176 - 136 * shard, 1)
        b = sums if shard == 0 else pltpu.roll(sums, 1024 - 64 * shard, 1)
        block = jnp.where(first_row, a[:, 0:256], b[:, 0:256])
        block = jnp.concatenate([block, jnp.zeros((8, 256), f32)], axis=0).astype(bf16)
        packed[1, slot_of(1, shard, y, x), 112:128, 768:1024] = block

    order = (8, 9, 10, 11, 4, 12, 5, 13, 6, 14, 7, 15, 0, 1, 2, 3)

    @pl.when(core == 0)
    def _():
        for slot in order:
            copy(1, slot).start()

    transposed(flipped, crossed)

    def first(i, c):
        m = dot(flipped[slice(272 * i, 272 * i + 272), :], delta_first[...])
        for k in range(2):
            slot = slot_of(0, i * 2 + k, y, x)
            d = jnp.concatenate([m[136 * k : 136 * k + 136], jnp.zeros((8, WIDE), f32)], axis=0)
            packed[0, slot] = d.astype(bf16)
        return c

    for i in range(8):
        first(i, 0)

    @pl.when(core == 1)
    def _():
        for slot in order:
            copy(0, slot).start()

    cut = 80

    def ring1(j):
        return ring(
            lambda d: packed.at[core, d * 4 + j],
            cut,
            PIECE,
            (via_plus.at[j], via_minus.at[j]),
            (packed.at[core, 4 + j, pl.ds(0, cut)], packed.at[core, 12 + j, pl.ds(cut, PIECE - cut)]),
            (got_plus.at[j], got_minus.at[j]),
            send1.at[j],
            recv1.at[j],
            first_peer(1),
            first_peer(3),
        )

    def add_pair(slot):
        copy(1 - core, slot).wait_recv()
        packed[core, slot] = (packed[core, slot].astype(f32) + landed[slot].astype(f32)).astype(bf16)

    def go_far(j, c):
        add_pair(8 + j)
        go(ring1(j), 0, 1)
        return c

    lax.fori_loop(0, 4, go_far, 0)

    def go_near(j, c):
        add_pair(4 + j)
        go(ring1(j), 2)
        add_pair(12 + j)
        go(ring1(j), 3)
        return c

    lax.fori_loop(0, 4, go_near, 0)

    def go_on(j, c):
        arrived(ring1(j), 0, 1)
        low, high = pl.ds(0, cut), pl.ds(cut, PIECE - cut)
        packed[core, 4 + j, low] = (
            packed[core, 4 + j, low].astype(f32) + via_plus[j].astype(f32)
        ).astype(bf16)
        packed[core, 12 + j, high] = (
            packed[core, 12 + j, high].astype(f32) + via_minus[j].astype(f32)
        ).astype(bf16)
        go(ring1(j), 4, 5)
        return c

    lax.fori_loop(0, 4, go_on, 0)

    def keep(j, c):
        add_pair(j)
        return c

    lax.fori_loop(0, 4, keep, 0)

    def finish(j, c):
        arrived(ring1(j), 2, 3, 4, 5)
        total = packed[core, j].astype(f32) + got_plus[j].astype(f32) + got_minus[j].astype(f32)
        out[j] = total.astype(bf16)
        return c

    lax.fori_loop(0, 4, finish, 0)

    def drain(slot, c):
        copy(1 - core, slot).wait_send()
        return c

    lax.fori_loop(0, 16, drain, 0)

    def drain1(j, c):
        for k in range(6):
            ring1(j)(k).wait_send()
        return c

    lax.fori_loop(0, 4, drain1, 0)
    own_table().wait()
    for d in range(1, n_table):
        came_table(d).wait_recv()
        exchange_table(d).wait_send()


def dense_part(big, rows):
    vmem = pl.BlockSpec(memory_space=pltpu.VMEM)
    anywhere = pl.BlockSpec(memory_space=pl.ANY)
    n_table = 2 * Z
    dma = pltpu.SemaphoreType.DMA
    return pl.pallas_call(
        dense_kernel,
        out_shape=(
            jax.ShapeDtypeStruct((n_table, 256, 128), bf16),
            jax.ShapeDtypeStruct((4, PIECE, WIDE), bf16),
        ),
        in_specs=[anywhere] * 6 + [vmem] * 5,
        out_specs=(anywhere, vmem),
        scratch_shapes=[
            pltpu.VMEM((256, 2176), bf16),
            pltpu.VMEM((2176, 256), bf16),
            pltpu.VMEM((256, 2176), bf16),
            pltpu.VMEM((2176, 1024), bf16),
            pltpu.VMEM((1024, 1024), bf16),
            pltpu.VMEM((256, 2176), f32),
            pltpu.VMEM((256, 2176), bf16),
            pltpu.VMEM((256, 1024), f32),
            pltpu.VMEM((256, 1024), f32),
            pltpu.VMEM((256, 1024), bf16),
            pltpu.VMEM((256, 1024), bf16),
            pltpu.VMEM((256, 1024), bf16),
            pltpu.VMEM((256, 1024), bf16),
            pltpu.VMEM((256, 2176), f32),
            pltpu.VMEM((256, 2176), bf16),
            pltpu.VMEM((256, 256), bf16),
            pltpu.VMEM((256, 256), bf16),
            pltpu.VMEM((1, 1024), f32),
            pltpu.VMEM((n_table + 1, 256, 128), bf16),
            pltpu.VMEM((2, 16, PIECE, WIDE), bf16),
            pltpu.VMEM((16, PIECE, WIDE), bf16),
            pltpu.VMEM((2176, 256), bf16),
            pltpu.VMEM((256, 256), bf16),
            pltpu.VMEM((4, 80, WIDE), bf16),
            pltpu.VMEM((4, 64, WIDE), bf16),
            pltpu.VMEM((4, PIECE, WIDE), bf16),
            pltpu.VMEM((4, PIECE, WIDE), bf16),
            dma((10,)),
            dma((n_table - 1,)),
            dma((n_table - 1,)),
            dma((16,)),
            dma((16,)),
            dma((4, 6)),
            dma((4, 6)),
            dma,
        ],
        compiler_params=pltpu.CompilerParams(
            collective_id=0, has_side_effects=True, vmem_limit_bytes=58 << 20
        ),
    )(*big, *rows)


def blocks(count, size, body):
    for i in range(count):
        body(slice(i * size, i * size + size))


def exchange_kernel(
    parts,
    dense_mid,
    row_out,
    h1_out,
    h2_out,
    up_out,
    down_out,
    vec_out,
    via_plus,
    via_minus,
    acc_plus,
    acc_minus,
    got_plus,
    got_minus,
    mid,
    via2,
    got2,
    dense_via_plus,
    dense_via_minus,
    dense_acc_plus,
    dense_acc_minus,
    dense_got,
    zparts,
    zgot,
    final,
    send1,
    recv1,
    send2,
    recv2,
    wsend,
    wrecv,
    zsend,
    zrecv,
    gsend,
    grecv,
    csend,
    crecv,
):
    table, row, core, z, y, x = place()
    sibling = z * 2 + 1 - core
    rows = parts.shape[1]

    def first_peer(d):
        return (table, shard_of(core, y, x, d, 0))

    def second_peer(j):
        return (table, shard_of(core, y, x, 0, j))

    def z_peer(d):
        return (lax.rem(z + d, Z) * 2 + core, row)

    barrier = pltpu.get_barrier_semaphore()
    peers = [first_peer(1), first_peer(3), second_peer(1), second_peer(3)]
    peers += [z_peer(d) for d in range(1, Z)] + [(sibling, row)]
    for who in peers:
        pl.semaphore_signal(barrier, inc=1, device_id=who, device_id_type=MESH)
    pl.semaphore_wait(barrier, len(peers))

    half = rows // 2

    def ring1(j):
        return ring(
            lambda d: parts.at[shard_of(core, y, x, d, j)],
            half,
            rows,
            (via_plus.at[j], via_minus.at[j]),
            (acc_plus.at[j], acc_minus.at[j]),
            (got_plus.at[j], got_minus.at[j]),
            send1.at[j],
            recv1.at[j],
            first_peer(1),
            first_peer(3),
        )

    def ring2():
        return ring(
            lambda d: mid.at[d],
            half,
            rows,
            (via2.at[0], via2.at[1]),
            (mid.at[1, pl.ds(0, half)], mid.at[3, pl.ds(half, half)]),
            (got2.at[0], got2.at[1]),
            send2,
            recv2,
            second_peer(1),
            second_peer(3),
        )

    cut = 80

    def ringw():
        return ring(
            lambda d: dense_mid.at[d],
            cut,
            PIECE,
            (dense_via_plus, dense_via_minus),
            (dense_acc_plus, dense_acc_minus),
            (dense_got.at[0], dense_got.at[1]),
            wsend,
            wrecv,
            second_peer(1),
            second_peer(3),
        )

    def copyz(d):
        return remote(
            zparts.at[lax.rem(z + d, Z)], zgot.at[d - 1], zsend.at[d - 1], zrecv.at[d - 1], z_peer(d)
        )

    def copyg(d, which):
        piece = final.at[core, which]
        return remote(piece, piece, gsend.at[d - 1], grecv.at[d - 1], z_peer(d))

    def copyc(half):
        return remote(final.at[half], final.at[half], csend, crecv, (sibling, row))

    def add_up(*terms):
        total = terms[0].astype(f32)
        for term in terms[1:]:
            total = total + term.astype(f32)
        return total

    def forward(j):
        to_plus, to_minus = shard_of(core, y, x, 1, j), shard_of(core, y, x, 3, j)
        copies = ring1(j)
        arrived(copies, 0)

        def plus(at):
            acc_plus[j, at, :] = add_up(parts[to_plus, at, :], via_plus[j, at, :]).astype(bf16)

        blocks(half // 128, 128, plus)
        go(copies, 4)
        arrived(copies, 1)

        def minus(at):
            later = slice(half + at.start, half + at.stop)
            acc_minus[j, at, :] = add_up(parts[to_minus, later, :], via_minus[j, at, :]).astype(bf16)

        blocks(half // 128, 128, minus)
        go(copies, 5)

    def row_mid(j):
        arrived(ring1(j), 2, 3, 4, 5)
        mine = shard_of(core, y, x, 0, j)

        def block(at):
            total = add_up(parts[mine, at, :], got_plus[j, at, :], got_minus[j, at, :])
            mid[j, at, :] = total.astype(bf16)

        blocks(rows // 128, 128, block)

    go(ringw(), 0, 1)
    go(ring1(2), 0, 1)
    go(ringw(), 2, 3)
    go(ring1(2), 2, 3)
    go(ring1(1), 0, 1)
    arrived(ringw(), 0, 1)

    def dense_plus(at):
        dense_acc_plus[at, :] = add_up(dense_mid[1, at, :], dense_via_plus[at, :]).astype(bf16)

    def dense_minus(at):
        later = slice(cut + at.start, cut + at.stop)
        dense_acc_minus[at, :] = add_up(dense_mid[3, later, :], dense_via_minus[at, :]).astype(bf16)

    blocks(cut // 16, 16, dense_plus)
    blocks((PIECE - cut) // 16, 16, dense_minus)
    go(ringw(), 4, 5)
    forward(2)
    go(ring1(1), 2, 3)
    go(ring1(3), 0, 1)
    forward(1)
    go(ring1(3), 2, 3)
    go(ring1(0), 0, 1)
    arrived(ringw(), 2, 3, 4, 5)

    def dense_last(at):
        total = add_up(dense_mid[0, at, :], dense_got[0, at, :], dense_got[1, at, :]).astype(bf16)
        for k in range(Z):
            zparts[k, at, :] = total[:, 128 * k : 128 * k + 128]

    blocks(PIECE // 16, 16, dense_last)
    for d in range(1, Z):
        copyz(d).start()
    forward(3)
    go(ring1(0), 2, 3)
    for d in range(1, Z):
        copyz(d).wait_recv()
    final[core, z] = add_up(zparts[z], *[zgot[d - 1] for d in range(1, Z)]).astype(bf16)
    for d in range(1, Z):
        copyg(d, z).start()
    row_mid(2)
    go(ring2(), 0, 1)
    forward(0)
    row_mid(1)
    go(ring2(), 2)
    for d in range(1, Z):
        copyg(d, lax.rem(z - d + Z, Z)).wait_recv()
    copyc(core).start()
    row_mid(3)
    go(ring2(), 3)
    arrived(ring2(), 0, 1)

    def mid_add(at):
        later = slice(half + at.start, half + at.stop)
        mid[1, at, :] = add_up(mid[1, at, :], via2[0, at, :]).astype(bf16)
        mid[3, later, :] = add_up(mid[3, later, :], via2[1, at, :]).astype(bf16)

    blocks(half // 128, 128, mid_add)
    go(ring2(), 4, 5)
    copyc(1 - core).wait_recv()
    for k in range(Z):
        at = slice(128 * k, 128 * k + 128)
        h1_out[:, at] = final[0, k, :, :].astype(f32)[0:136]
        h2_out[:, at] = final[1, k, 0:64, :].astype(f32)
        up_out[:, at] = final[1, k, 64:80, :].astype(f32)
        up_out[:, 1024 + 128 * k : 1024 + 128 * k + 128] = final[1, k, 80:96, :].astype(f32)
    up_out[:, 2048:2176] = final[1, 6, 96:112, :].astype(f32)
    for k in range(2):
        at = slice(128 * k, 128 * k + 128)
        down_out[0:48, at] = final[1, k, 96:144, :].astype(f32)
        down_out[48:96, at] = final[1, 2 + k, 96:144, :].astype(f32)
        down_out[96:136, at] = final[1, 4 + k, 96:144, :].astype(f32)[0:40]
        vec_out[:, at] = final[1, 6 + k, 112:128, :].astype(f32)[0:8]
    arrived(ring1(0), 2, 3, 4, 5)
    arrived(ring2(), 2, 3, 4, 5)

    own = shard_of(core, y, x, 0, 0)

    def row_last(at):
        row_out[at, :] = add_up(
            parts[own, at, :],
            got_plus[0, at, :],
            got_minus[0, at, :],
            got2[0, at, :],
            got2[1, at, :],
        )

    blocks(rows // 128, 128, row_last)

    for j in range(4):
        for k in range(6):
            ring1(j)(k).wait_send()
    for k in range(6):
        ring2()(k).wait_send()
        ringw()(k).wait_send()
    for d in range(1, Z):
        copyz(d).wait_send()
        copyg(d, z).wait_send()
    copyc(core).wait_send()


def exchange(parts, sums):
    vmem = pl.BlockSpec(memory_space=pltpu.VMEM)
    rows, width = parts.shape[1:]
    half = rows // 2
    dma = pltpu.SemaphoreType.DMA
    return pl.pallas_call(
        exchange_kernel,
        out_shape=(
            jax.ShapeDtypeStruct((rows, width), f32),
            jax.ShapeDtypeStruct((136, 1024), f32),
            jax.ShapeDtypeStruct((64, 1024), f32),
            jax.ShapeDtypeStruct((16, 2176), f32),
            jax.ShapeDtypeStruct((136, 256), f32),
            jax.ShapeDtypeStruct((8, 256), f32),
        ),
        in_specs=[vmem] * 2,
        out_specs=(vmem,) * 6,
        scratch_shapes=[
            pltpu.VMEM((4, half, width), bf16),
            pltpu.VMEM((4, half, width), bf16),
            pltpu.VMEM((4, half, width), bf16),
            pltpu.VMEM((4, half, width), bf16),
            pltpu.VMEM((4, rows, width), bf16),
            pltpu.VMEM((4, rows, width), bf16),
            pltpu.VMEM((4, rows, width), bf16),
            pltpu.VMEM((2, half, width), bf16),
            pltpu.VMEM((2, rows, width), bf16),
            pltpu.VMEM((80, WIDE), bf16),
            pltpu.VMEM((64, WIDE), bf16),
            pltpu.VMEM((80, WIDE), bf16),
            pltpu.VMEM((64, WIDE), bf16),
            pltpu.VMEM((2, PIECE, WIDE), bf16),
            pltpu.VMEM((Z, PIECE, 128), bf16),
            pltpu.VMEM((Z - 1, PIECE, 128), bf16),
            pltpu.VMEM((2, Z, PIECE, 128), bf16),
            dma((4, 6)),
            dma((4, 6)),
            dma((6,)),
            dma((6,)),
            dma((6,)),
            dma((6,)),
            dma((Z - 1,)),
            dma((Z - 1,)),
            dma((Z - 1,)),
            dma((Z - 1,)),
            dma,
            dma,
        ],
        compiler_params=pltpu.CompilerParams(
            collective_id=1, has_side_effects=True, vmem_limit_bytes=40 << 20
        ),
    )(parts, sums)


def scatter_kernel(slots_ref, v_ref, o_ref, s_ref, wide, sem, *accs):
    count = v_ref.shape[0]
    slots, width = o_ref.shape
    row = lax.axis_index("row")
    per_table = slots_ref.shape[1] // (2 * Z)
    own = per_table // (Y * X)

    def fetch(t):
        at = (t // 2) * per_table + row * own + (t % 2) * 128
        return pltpu.make_async_copy(
            slots_ref.at[:, pl.ds(pl.multiple_of(at, 128), 128)], s_ref.at[t], sem.at[t]
        )

    for t in range(count // 128):
        fetch(t).start()

    def clear(i, c):
        for acc in accs:
            acc[pl.ds(pl.multiple_of(i * 256, 256), 256), :] = jnp.zeros((256, width), f32)
        return c

    lax.fori_loop(0, slots // 256, clear, 0)
    wide[...] = v_ref[...].astype(f32)
    for t in range(count // 128):
        fetch(t).wait()

    def step(g, c):
        for i in range(0, 128, 2):
            row0 = wide[pl.ds(g * 128 + i, 1), :]
            row1 = wide[pl.ds(g * 128 + i + 1, 1), :]
            for which, acc in enumerate(accs):
                slot0 = s_ref[g, which, i]
                slot1 = s_ref[g, which, i + 1]
                old0 = acc[pl.ds(slot0, 1), :]
                old1 = acc[pl.ds(slot1, 1), :]
                new0 = old0 + row0
                new1 = jnp.where(slot0 == slot1, new0, old1) + row1
                acc[pl.ds(slot0, 1), :] = new0
                acc[pl.ds(slot1, 1), :] = new1
        return c

    lax.fori_loop(0, count // 128, step, 0)

    def finish(i, c):
        at = pl.ds(pl.multiple_of(i * 128, 128), 128)
        total = accs[0][at, :]
        for acc in accs[1:]:
            total = total + acc[at, :]
        o_ref[at, :] = total.astype(o_ref.dtype)
        return c

    lax.fori_loop(0, slots // 128, finish, 0)


def scatter_rows(slots, values, total_slots):
    count, width = values.shape
    hot = slots.shape[0]
    return pl.pallas_call(
        scatter_kernel,
        out_shape=jax.ShapeDtypeStruct((total_slots, width), bf16),
        in_specs=[pl.BlockSpec(memory_space=pl.ANY), pl.BlockSpec(memory_space=pltpu.VMEM)],
        out_specs=pl.BlockSpec(memory_space=pltpu.VMEM),
        scratch_shapes=[
            pltpu.SMEM((count // 128, hot, 128), jnp.int32),
            pltpu.VMEM((count, width), f32),
            pltpu.SemaphoreType.DMA((count // 128,)),
        ]
        + [pltpu.VMEM((total_slots, width), f32)] * hot,
        compiler_params=pltpu.CompilerParams(vmem_limit_bytes=44 << 20),
        cost_estimate=pl.CostEstimate(
            flops=10_000_000, bytes_accessed=100_000_000, transcendentals=0
        ),
    )(slots, values)


def local(
    dense_feat,
    pooled,
    labels,
    cross_down,
    cross_up,
    cross_bias,
    w_hidden1,
    bias1,
    w_hidden2,
    bias2,
    w_logit,
    lookup_slots,
):
    width = dense_feat.shape[1]
    n_row = lax.axis_size("row")
    u_shard = 1024
    big = (dense_feat, pooled, cross_down, cross_up, w_hidden1, w_hidden2)
    rows = [one[None, :] for one in (labels, cross_bias, bias1, bias2, w_logit)]
    received, sums = dense_part(big, rows)
    partial = scatter_rows(
        jnp.transpose(lookup_slots[0]), received.reshape(-1, width), n_row * u_shard
    )
    row_grads, g_h1, g_h2, g_up, g_down, vecs = exchange(
        partial.reshape(n_row, u_shard, width), sums
    )
    return (
        row_grads[None],
        g_down,
        g_up,
        vecs[0, 0:136],
        g_h1,
        vecs[1, 0:64],
        g_h2,
        vecs[2, 0:64],
        vecs[3, 0:64],
    )


def solution(mesh):
    in_specs = (
        P(("table", "row"), None),
        P(("table", "row"), None),
        P(("table", "row")),
        P(),
        P(),
        P(),
        P(),
        P(),
        P(),
        P(),
        P(),
        P("table", None, None),
    )
    out_specs = (
        P("table", "row", None),
        P("row", None),
        P("row", None),
        P("row"),
        P("row", None),
        P("row"),
        P("row", None),
        P("row"),
        P("row"),
    )
    return jax.shard_map(local, mesh=mesh, in_specs=in_specs, out_specs=out_specs, check_vma=False)
```

time: 135 us -> 116 us (0.86)
  the two profiles are of different devices: /device:TPU:1 before, /device:TPU:2 now
where the time goes in v4:
time: 116 us; the launch traced here: 114 us
  Pallas kernels  106 us (91%)
  local copies, waits for them, and re-layouts  7.24 us (6%)
    pallas_call x1, Pallas kernels, exchange(): pl.pallas_call(exchange_kernel, out_shape=(jax.ShapeDtypeStruct((rows, wi...  41.9 us
    pallas_call x1, Pallas kernels, dense_part(): pl.pallas_call(dense_kernel, out_shape=(jax.ShapeDtypeStruct((n_table, 25...  39.6 us
    pallas_call x1, Pallas kernels, scatter_rows(): pl.pallas_call(scatter_kernel, out_shape=jax.ShapeDtypeStruct((total_slot...  24.7 us
    unnamed x11, local copies, waits for them, and re-layouts  4.84 us

profile of v4, /device:TPU:2, one launch (start us, length us, event | category | flops | bytes accessed | tf_op | source)
XLA Modules:
  0.0 114.1 jit_solution(10982648995708508291)
XLA Ops:
  0.6 1.3 %broadcast_in_dim.19.cross_bias = f32[1,2176]{1,0:T(1,128)} reshape(f32[2176]{0:T(1024)} %param.17) | data formatting | bytes 17408 | tf_op jit(solution)/shard_map/broadcast_in_dim | solution.py:895
  2.0 0.0 copy-start.1
  2.0 39.6 %shard_map.187 = (bf16[16,256,128]{2,1,0:T(8,128)(2,1)}, bf16[4,144,1024]{2,1,0:T(8,128)(2,1)}) custom-call(bf16[256,128]{1,0:T(8,128)(2,1)} %dense_feat.1, bf16[256,2048]{1,0:T(8,128)(2,1)} %pooled.1, bf16[2176,256]{1,0:T(8,128)(2,1)} %cross_down.1, bf16[256,2176]{1,0:T(8,128)(2,1)} %cross_up.1, bf16[2176,1024]{1,0:T(8,128)(2,1)} %w_hidden1.1, ...), custom_call_target="tpu_custom_call" | custom-call | tf_op jit(solution)/shard_map/pallas_call | solution.py:439
  41.6 0.0 copy-done.1
  41.6 0.0 copy-start.2
  41.6 1.2 %copy-done.2 = bf16[16,256,128]{2,1,0:T(8,128)(2,1)S(1)} copy-done((bf16[16,256,128]{2,1,0:T(8,128)(2,1)S(1)}, bf16[16,256,128]{2,1,0:T(8,128)(2,1)}, u32[]{:S(2)}) %copy-start.2) | copy-done | bytes 1048600
  42.8 0.0 copy-start
  42.8 24.7 %shard_map.188 = bf16[16384,128]{1,0:T(8,128)(2,1)S(1)} custom-call(s32[4,65536]{1,0:T(4,128)S(1)} %bitcast.18, bf16[4096,128]{1,0:T(8,128)(2,1)S(1)} %bitcast.19), custom_call_target="tpu_custom_call" | custom-call | flops 10000000 | bytes 100000000 | tf_op jit(solution)/shard_map/pallas_call | solution.py:859
  67.5 0.0 copy-done
  67.5 41.9 %shard_map.189 = (f32[1024,128]{1,0:T(8,128)S(1)}, f32[136,1024]{1,0:T(8,128)S(1)}, f32[64,1024]{1,0:T(8,128)S(1)}, f32[16,2176]{1,0:T(8,128)S(1)}, f32[136,256]{1,0:T(8,128)S(1)}, /*index=5*/f32[8,256]{1,0:T(8,128)S(1)}) custom-call(bf16[16,1024,128]{2,1,0:T(8,128)(2,1)S(1)} %bitcast.17, bf16[4,144,1024]{2,1,0:T(8,128)(2,1)S(1)} %copy-done), custom_call_target="tpu_custom_call" | custom-call | tf_op jit(solution)/shard_map/pallas_call | solution.py:753
  109.4 0.6 slice.12
  110.0 0.5 slice_bitcast_fusion
  110.5 0.8 copy.26
  111.3 0.7 copy.27
  112.0 0.7 copy.28
  112.6 0.8 copy.29
  113.4 0.7 copy.30
Async XLA Ops:
  2.0 39.6 %copy-start.1 = (s32[1,65536,4]{1,2,0:T(4,128)S(1)}, s32[1,65536,4]{1,2,0:T(4,128)}, u32[]{:S(2)}) copy-start(s32[1,65536,4]{1,2,0:T(4,128)} %param.23) | copy-start | bytes 3145732
  41.6 1.2 %copy-start.2 = (bf16[16,256,128]{2,1,0:T(8,128)(2,1)S(1)}, bf16[16,256,128]{2,1,0:T(8,128)(2,1)}, u32[]{:S(2)}) copy-start(bf16[16,256,128]{2,1,0:T(8,128)(2,1)} %get-tuple-element.17) | copy-start | bytes 3145732
  42.8 24.7 %copy-start = (bf16[4,144,1024]{2,1,0:T(8,128)(2,1)S(1)}, bf16[4,144,1024]{2,1,0:T(8,128)(2,1)}, u32[]{:S(2)}) copy-start(bf16[4,144,1024]{2,1,0:T(8,128)(2,1)} %get-tuple-element.18.dense_mid) | copy-start | bytes 3538948

commit v5 on v4

--- a/solution.py
+++ b/solution.py
@@ -190,7 +190,7 @@
     loads[3].wait()
 
     def cross(at, i):
-        widened = dot(reduced[...], up_w[:, at]) + cross_bias[:, at]
+        widened = dot(reduced[...], up_w[:, at]) + cross_bias[at][None, :]
         base = stacked[:, at].astype(f32)
         crossed[:, at] = (base * widened + base).astype(bf16)
         wide_plus[:, at] = widened + 1.0
@@ -496,11 +496,7 @@
     parts,
     dense_mid,
     row_out,
-    h1_out,
-    h2_out,
-    up_out,
-    down_out,
-    vec_out,
+    final,
     via_plus,
     via_minus,
     acc_plus,
@@ -517,7 +513,8 @@
     dense_got,
     zparts,
     zgot,
-    final,
+    own,
+    own_sem,
     send1,
     recv1,
     send2,
@@ -615,31 +612,39 @@
             total = total + term.astype(f32)
         return total
 
+    def local(k, j):
+        src, dst = (
+            (parts.at[shard_of(core, y, x, 1, j), pl.ds(0, half)], acc_plus.at[j]),
+            (parts.at[shard_of(core, y, x, 3, j), pl.ds(half, half)], acc_minus.at[j]),
+            (parts.at[shard_of(core, y, x, 0, j)], own.at[j]),
+        )[k]
+        return pltpu.make_async_copy(src, dst, own_sem.at[k, j])
+
     def forward(j):
-        to_plus, to_minus = shard_of(core, y, x, 1, j), shard_of(core, y, x, 3, j)
         copies = ring1(j)
+        local(0, j).wait()
         arrived(copies, 0)
 
         def plus(at):
-            acc_plus[j, at, :] = add_up(parts[to_plus, at, :], via_plus[j, at, :]).astype(bf16)
+            acc_plus[j, at, :] = add_up(acc_plus[j, at, :], via_plus[j, at, :]).astype(bf16)
 
         blocks(half // 128, 128, plus)
         go(copies, 4)
+        local(1, j).wait()
         arrived(copies, 1)
 
         def minus(at):
-            later = slice(half + at.start, half + at.stop)
-            acc_minus[j, at, :] = add_up(parts[to_minus, later, :], via_minus[j, at, :]).astype(bf16)
+            acc_minus[j, at, :] = add_up(acc_minus[j, at, :], via_minus[j, at, :]).astype(bf16)
 
         blocks(half // 128, 128, minus)
         go(copies, 5)
 
     def row_mid(j):
+        local(2, j).wait()
         arrived(ring1(j), 2, 3, 4, 5)
-        mine = shard_of(core, y, x, 0, j)
 
         def block(at):
-            total = add_up(parts[mine, at, :], got_plus[j, at, :], got_minus[j, at, :])
+            total = add_up(own[j, at, :], got_plus[j, at, :], got_minus[j, at, :])
             mid[j, at, :] = total.astype(bf16)
 
         blocks(rows // 128, 128, block)
@@ -649,6 +654,9 @@
     go(ringw(), 2, 3)
     go(ring1(2), 2, 3)
     go(ring1(1), 0, 1)
+    for j in (2, 1, 3, 0):
+        for k in range(3):
+            local(k, j).start()
     arrived(ringw(), 0, 1)
 
     def dense_plus(at):
@@ -704,6 +712,48 @@
     blocks(half // 128, 128, mid_add)
     go(ring2(), 4, 5)
     copyc(1 - core).wait_recv()
+    arrived(ring1(0), 2, 3, 4, 5)
+    arrived(ring2(), 2, 3, 4, 5)
+
+    local(2, 0).wait()
+
+    def row_last(at):
+        row_out[at, :] = add_up(
+            own[0, at, :],
+            got_plus[0, at, :],
+            got_minus[0, at, :],
+            got2[0, at, :],
+            got2[1, at, :],
+        )
+
+    blocks(rows // 128, 128, row_last)
+
+    for j in range(4):
+        for k in range(6):
+            ring1(j)(k).wait_send()
+    for k in range(6):
+        ring2()(k).wait_send()
+        ringw()(k).wait_send()
+    for d in range(1, Z):
+        copyz(d).wait_send()
+        copyg(d, z).wait_send()
+    copyc(core).wait_send()
+
+
+def unpack_kernel(
+    final,
+    rows,
+    row_out,
+    down_out,
+    up_out,
+    cross_bias_out,
+    h1_out,
+    bias1_out,
+    h2_out,
+    bias2_out,
+    logit_out,
+):
+    row_out[0] = rows[...]
     for k in range(Z):
         at = slice(128 * k, 128 * k + 128)
         h1_out[:, at] = final[0, k, :, :].astype(f32)[0:136]
@@ -716,33 +766,25 @@
         down_out[0:48, at] = final[1, k, 96:144, :].astype(f32)
         down_out[48:96, at] = final[1, 2 + k, 96:144, :].astype(f32)
         down_out[96:136, at] = final[1, 4 + k, 96:144, :].astype(f32)[0:40]
-        vec_out[:, at] = final[1, 6 + k, 112:128, :].astype(f32)[0:8]
-    arrived(ring1(0), 2, 3, 4, 5)
-    arrived(ring2(), 2, 3, 4, 5)
-
-    own = shard_of(core, y, x, 0, 0)
-
-    def row_last(at):
-        row_out[at, :] = add_up(
-            parts[own, at, :],
-            got_plus[0, at, :],
-            got_minus[0, at, :],
-            got2[0, at, :],
-            got2[1, at, :],
-        )
-
-    blocks(rows // 128, 128, row_last)
-
-    for j in range(4):
-        for k in range(6):
-            ring1(j)(k).wait_send()
-    for k in range(6):
-        ring2()(k).wait_send()
-        ringw()(k).wait_send()
-    for d in range(1, Z):
-        copyz(d).wait_send()
-        copyg(d, z).wait_send()
-    copyc(core).wait_send()
+    low = final[1, 6, 112:128, :].astype(f32)
+    high = final[1, 7, 112:128, :].astype(f32)
+    cross_bias_out[pl.ds(0, 128)] = low[0]
+    cross_bias_out[pl.ds(128, 8)] = high[0, 0:8]
+    for k, one in enumerate((bias1_out, bias2_out, logit_out)):
+        one[...] = low[k + 1, 0:64]
+
+
+def unpack(final, rows):
+    vmem = pl.BlockSpec(memory_space=pltpu.VMEM)
+    shapes = ((1,) + rows.shape, (136, 256), (16, 2176), (136,), (136, 1024), (64,), (64, 1024))
+    shapes += ((64,), (64,))
+    return pl.pallas_call(
+        unpack_kernel,
+        out_shape=tuple(jax.ShapeDtypeStruct(shape, f32) for shape in shapes),
+        in_specs=[vmem] * 2,
+        out_specs=(vmem,) * 9,
+        compiler_params=pltpu.CompilerParams(vmem_limit_bytes=16 << 20),
+    )(final, rows)
 
 
 def exchange(parts, sums):
@@ -754,14 +796,10 @@
         exchange_kernel,
         out_shape=(
             jax.ShapeDtypeStruct((rows, width), f32),
-            jax.ShapeDtypeStruct((136, 1024), f32),
-            jax.ShapeDtypeStruct((64, 1024), f32),
-            jax.ShapeDtypeStruct((16, 2176), f32),
-            jax.ShapeDtypeStruct((136, 256), f32),
-            jax.ShapeDtypeStruct((8, 256), f32),
+            jax.ShapeDtypeStruct((2, Z, PIECE, 128), bf16),
         ),
-        in_specs=[vmem] * 2,
-        out_specs=(vmem,) * 6,
+        in_specs=[pl.BlockSpec(memory_space=pl.ANY), vmem],
+        out_specs=(vmem,) * 2,
         scratch_shapes=[
             pltpu.VMEM((4, half, width), bf16),
             pltpu.VMEM((4, half, width), bf16),
@@ -779,7 +817,8 @@
             pltpu.VMEM((2, PIECE, WIDE), bf16),
             pltpu.VMEM((Z, PIECE, 128), bf16),
             pltpu.VMEM((Z - 1, PIECE, 128), bf16),
-            pltpu.VMEM((2, Z, PIECE, 128), bf16),
+            pltpu.VMEM((4, rows, width), bf16),
+            dma((3, 4)),
             dma((4, 6)),
             dma((4, 6)),
             dma((6,)),
@@ -794,17 +833,21 @@
             dma,
         ],
         compiler_params=pltpu.CompilerParams(
-            collective_id=1, has_side_effects=True, vmem_limit_bytes=40 << 20
+            collective_id=1, has_side_effects=True, vmem_limit_bytes=61 << 20
         ),
     )(parts, sums)
 
 
-def scatter_kernel(slots_ref, v_ref, o_ref, s_ref, wide, sem, *accs):
-    count = v_ref.shape[0]
-    slots, width = o_ref.shape
+def scatter_kernel(
+    slots_ref, values_ref, o_ref, s_ref, narrow, wide, done, sem, value_sem, out_sem, *accs
+):
+    count, width = wide.shape
+    slots = o_ref.shape[0]
     row = lax.axis_index("row")
     per_table = slots_ref.shape[1] // (2 * Z)
     own = per_table // (Y * X)
+    values = pltpu.make_async_copy(values_ref, narrow, value_sem)
+    values.start()
 
     def fetch(t):
         at = (t // 2) * per_table + row * own + (t % 2) * 128
@@ -817,57 +860,67 @@
 
     def clear(i, c):
         for acc in accs:
-            acc[pl.ds(pl.multiple_of(i * 256, 256), 256), :] = jnp.zeros((256, width), f32)
-        return c
-
-    lax.fori_loop(0, slots // 256, clear, 0)
-    wide[...] = v_ref[...].astype(f32)
+            acc[pl.ds(pl.multiple_of(i * 512, 512), 512), :] = jnp.zeros((512, width), f32)
+        return c
+
+    lax.fori_loop(0, slots // 512, clear, 0)
+    values.wait()
+    wide[...] = narrow[...].astype(f32)
     for t in range(count // 128):
         fetch(t).wait()
 
     def step(g, c):
-        for i in range(0, 128, 2):
-            row0 = wide[pl.ds(g * 128 + i, 1), :]
-            row1 = wide[pl.ds(g * 128 + i + 1, 1), :]
-            for which, acc in enumerate(accs):
-                slot0 = s_ref[g, which, i]
-                slot1 = s_ref[g, which, i + 1]
-                old0 = acc[pl.ds(slot0, 1), :]
-                old1 = acc[pl.ds(slot1, 1), :]
-                new0 = old0 + row0
-                new1 = jnp.where(slot0 == slot1, new0, old1) + row1
-                acc[pl.ds(slot0, 1), :] = new0
-                acc[pl.ds(slot1, 1), :] = new1
+        turn = 0
+        for i in range(128):
+            sample = wide[pl.ds(g * 128 + i, 1), :]
+            for which in range(s_ref.shape[1]):
+                acc = accs[turn % len(accs)]
+                turn += 1
+                at = pl.ds(s_ref[g, which, i], 1)
+                acc[at, :] = acc[at, :] + sample
         return c
 
     lax.fori_loop(0, count // 128, step, 0)
 
+    def leave(i):
+        at = pl.ds(pl.multiple_of(i * 1024, 1024), 1024)
+        return pltpu.make_async_copy(done.at[at], o_ref.at[at], out_sem.at[i])
+
     def finish(i, c):
-        at = pl.ds(pl.multiple_of(i * 128, 128), 128)
-        total = accs[0][at, :]
-        for acc in accs[1:]:
-            total = total + acc[at, :]
-        o_ref[at, :] = total.astype(o_ref.dtype)
-        return c
-
-    lax.fori_loop(0, slots // 128, finish, 0)
+        for part in range(2):
+            at = pl.ds(pl.multiple_of(i * 1024 + part * 512, 512), 512)
+            total = accs[0][at, :]
+            for acc in accs[1:]:
+                total = total + acc[at, :]
+            done[at, :] = total.astype(bf16)
+        leave(i).start()
+        return c
+
+    lax.fori_loop(0, slots // 1024, finish, 0)
+    for i in range(slots // 1024):
+        leave(i).wait()
 
 
 def scatter_rows(slots, values, total_slots):
     count, width = values.shape
     hot = slots.shape[0]
+    anywhere = pl.BlockSpec(memory_space=pl.ANY)
     return pl.pallas_call(
         scatter_kernel,
         out_shape=jax.ShapeDtypeStruct((total_slots, width), bf16),
-        in_specs=[pl.BlockSpec(memory_space=pl.ANY), pl.BlockSpec(memory_space=pltpu.VMEM)],
-        out_specs=pl.BlockSpec(memory_space=pltpu.VMEM),
+        in_specs=[anywhere, anywhere],
+        out_specs=anywhere,
         scratch_shapes=[
             pltpu.SMEM((count // 128, hot, 128), jnp.int32),
+            pltpu.VMEM((count, width), bf16),
             pltpu.VMEM((count, width), f32),
+            pltpu.VMEM((total_slots, width), bf16),
             pltpu.SemaphoreType.DMA((count // 128,)),
+            pltpu.SemaphoreType.DMA,
+            pltpu.SemaphoreType.DMA((total_slots // 1024,)),
         ]
-        + [pltpu.VMEM((total_slots, width), f32)] * hot,
-        compiler_params=pltpu.CompilerParams(vmem_limit_bytes=44 << 20),
+        + [pltpu.VMEM((total_slots, width), f32)] * 6,
+        compiler_params=pltpu.CompilerParams(vmem_limit_bytes=57 << 20),
         cost_estimate=pl.CostEstimate(
             flops=10_000_000, bytes_accessed=100_000_000, transcendentals=0
         ),
@@ -892,25 +945,13 @@
     n_row = lax.axis_size("row")
     u_shard = 1024
     big = (dense_feat, pooled, cross_down, cross_up, w_hidden1, w_hidden2)
-    rows = [one[None, :] for one in (labels, cross_bias, bias1, bias2, w_logit)]
+    rows = [labels[None, :], cross_bias, bias1[None, :], bias2[None, :], w_logit[None, :]]
     received, sums = dense_part(big, rows)
     partial = scatter_rows(
         jnp.transpose(lookup_slots[0]), received.reshape(-1, width), n_row * u_shard
     )
-    row_grads, g_h1, g_h2, g_up, g_down, vecs = exchange(
-        partial.reshape(n_row, u_shard, width), sums
-    )
-    return (
-        row_grads[None],
-        g_down,
-        g_up,
-        vecs[0, 0:136],
-        g_h1,
-        vecs[1, 0:64],
-        g_h2,
-        vecs[2, 0:64],
-        vecs[3, 0:64],
-    )
+    row_sums, final = exchange(partial.reshape(n_row, u_shard, width), sums)
+    return tuple(unpack(final, row_sums))
 
 
 def solution(mesh):

time: 116 us -> 112 us (0.966)
  the two profiles are of different devices: /device:TPU:2 before, /device:TPU:0 now
where the time goes in v5:
time: 112 us
  Pallas kernels  109 us (97%)
  local copies, waits for them, and re-layouts  2.1 us (2%)
    pallas_call x1, Pallas kernels, exchange(): pl.pallas_call(exchange_kernel, out_shape=(jax.ShapeDtypeStruct((rows, wi...  47.3 us
    pallas_call x1, Pallas kernels, dense_part(): pl.pallas_call(dense_kernel, out_shape=(jax.ShapeDtypeStruct((n_table, 25...  39.1 us
    pallas_call x1, Pallas kernels, scatter_rows(): pl.pallas_call(scatter_kernel, out_shape=jax.ShapeDtypeStruct((total_slot...  21.7 us

profile of v5, /device:TPU:0, one launch (start us, length us, event | category | flops | bytes accessed | tf_op | source)
XLA Modules:
  0.0 112.1 jit_solution(14309968818143395026)
XLA Ops:
  0.6 39.1 %shard_map.187 = (bf16[16,256,128]{2,1,0:T(8,128)(2,1)}, bf16[4,144,1024]{2,1,0:T(8,128)(2,1)}) custom-call(bf16[256,128]{1,0:T(8,128)(2,1)} %dense_feat.1, bf16[256,2048]{1,0:T(8,128)(2,1)} %pooled.1, bf16[2176,256]{1,0:T(8,128)(2,1)} %cross_down.1, bf16[256,2176]{1,0:T(8,128)(2,1)} %cross_up.1, bf16[2176,1024]{1,0:T(8,128)(2,1)} %w_hidden1.1, ...), custom_call_target="tpu_custom_call" | custom-call | tf_op jit(solution)/shard_map/pallas_call | solution.py:439
  39.7 21.7 %shard_map.188 = bf16[16384,128]{1,0:T(8,128)(2,1)} custom-call(s32[4,65536]{1,0:T(4,128)} %bitcast.10, bf16[4096,128]{1,0:T(8,128)(2,1)} %bitcast.11), custom_call_target="tpu_custom_call" | custom-call | flops 10000000 | bytes 100000000 | tf_op jit(solution)/shard_map/pallas_call | solution.py:908
  61.4 47.3 %shard_map.189 = (f32[1024,128]{1,0:T(8,128)}, bf16[2,8,144,128]{3,2,1,0:T(8,128)(2,1)}) custom-call(bf16[16,1024,128]{2,1,0:T(8,128)(2,1)} %bitcast.9, bf16[4,144,1024]{2,1,0:T(8,128)(2,1)} %get-tuple-element.14.dense_mid), custom_call_target="tpu_custom_call" | custom-call | tf_op jit(solution)/shard_map/pallas_call | solution.py:795
  108.7 0.0 copy-start
  108.7 1.1 copy-done
  109.8 0.0 copy-start.1
  109.8 1.0 copy-done.1
  110.8 1.3 %shard_map.190 = (f32[1,1024,128]{2,1,0:T(8,128)}, f32[136,256]{1,0:T(8,128)}, f32[16,2176]{1,0:T(8,128)}, f32[136]{0:T(256)}, f32[136,1024]{1,0:T(8,128)}, /*in...) custom-call(bf16[2,8,144,128]{3,2,1,0:T(8,128)(2,1)S(1)} %copy-done, f32[1024,128]{1,0:T(8,128)S(1)} %copy-done.1), custom_call_target="tpu_custom_call" | custom-call | tf_op jit(solution)/shard_map/pallas_call | solution.py:781
Async XLA Ops:
  108.7 1.1 copy-start
  109.8 1.0 copy-start.1

commit v6 on v5

--- a/solution.py
+++ b/solution.py
@@ -833,15 +833,13 @@
             dma,
         ],
         compiler_params=pltpu.CompilerParams(
-            collective_id=1, has_side_effects=True, vmem_limit_bytes=61 << 20
+            collective_id=1, has_side_effects=True, vmem_limit_bytes=40 << 20
         ),
     )(parts, sums)
 
 
-def scatter_kernel(
-    slots_ref, values_ref, o_ref, s_ref, narrow, wide, done, sem, value_sem, out_sem, *accs
-):
-    count, width = wide.shape
+def scatter_kernel(slots_ref, values_ref, o_ref, s_ref, narrow, wide, sem, value_sem, *accs):
+    count, width = narrow.shape
     slots = o_ref.shape[0]
     row = lax.axis_index("row")
     per_table = slots_ref.shape[1] // (2 * Z)
@@ -865,14 +863,14 @@
 
     lax.fori_loop(0, slots // 512, clear, 0)
     values.wait()
-    wide[...] = narrow[...].astype(f32)
     for t in range(count // 128):
         fetch(t).wait()
 
     def step(g, c):
+        wide[...] = narrow[pl.ds(pl.multiple_of(g * 128, 128), 128), :].astype(f32)
         turn = 0
         for i in range(128):
-            sample = wide[pl.ds(g * 128 + i, 1), :]
+            sample = wide[i : i + 1, :]
             for which in range(s_ref.shape[1]):
                 acc = accs[turn % len(accs)]
                 turn += 1
@@ -882,23 +880,15 @@
 
     lax.fori_loop(0, count // 128, step, 0)
 
-    def leave(i):
-        at = pl.ds(pl.multiple_of(i * 1024, 1024), 1024)
-        return pltpu.make_async_copy(done.at[at], o_ref.at[at], out_sem.at[i])
-
     def finish(i, c):
-        for part in range(2):
-            at = pl.ds(pl.multiple_of(i * 1024 + part * 512, 512), 512)
-            total = accs[0][at, :]
-            for acc in accs[1:]:
-                total = total + acc[at, :]
-            done[at, :] = total.astype(bf16)
-        leave(i).start()
-        return c
-
-    lax.fori_loop(0, slots // 1024, finish, 0)
-    for i in range(slots // 1024):
-        leave(i).wait()
+        at = pl.ds(pl.multiple_of(i * 512, 512), 512)
+        total = accs[0][at, :]
+        for acc in accs[1:]:
+            total = total + acc[at, :]
+        o_ref[at, :] = total.astype(bf16)
+        return c
+
+    lax.fori_loop(0, slots // 512, finish, 0)
 
 
 def scatter_rows(slots, values, total_slots):
@@ -907,20 +897,18 @@
     anywhere = pl.BlockSpec(memory_space=pl.ANY)
     return pl.pallas_call(
         scatter_kernel,
-        out_shape=jax.ShapeDtypeStruct((total_slots, width), bf16),
+        out_shape=pltpu.VMEM((total_slots, width), bf16),
         in_specs=[anywhere, anywhere],
-        out_specs=anywhere,
+        out_specs=pl.BlockSpec(memory_space=pltpu.VMEM),
         scratch_shapes=[
             pltpu.SMEM((count // 128, hot, 128), jnp.int32),
             pltpu.VMEM((count, width), bf16),
-            pltpu.VMEM((count, width), f32),
-            pltpu.VMEM((total_slots, width), bf16),
+            pltpu.VMEM((128, width), f32),
             pltpu.SemaphoreType.DMA((count // 128,)),
             pltpu.SemaphoreType.DMA,
-            pltpu.SemaphoreType.DMA((total_slots // 1024,)),
         ]
         + [pltpu.VMEM((total_slots, width), f32)] * 6,
-        compiler_params=pltpu.CompilerParams(vmem_limit_bytes=57 << 20),
+        compiler_params=pltpu.CompilerParams(vmem_limit_bytes=50 << 20),
         cost_estimate=pl.CostEstimate(
             flops=10_000_000, bytes_accessed=100_000_000, transcendentals=0
         ),

time: 112 us -> 107 us (0.955)
  the two profiles are of different devices: /device:TPU:0 before, /device:TPU:2 now
where the time goes in v6:
time: 107 us; the launch traced here: 105 us
  Pallas kernels  104 us (97%)
    pallas_call x1, Pallas kernels, exchange(): pl.pallas_call(exchange_kernel, out_shape=(jax.ShapeDtypeStruct((rows, wi...  42.1 us
    pallas_call x1, Pallas kernels, dense_part(): pl.pallas_call(dense_kernel, out_shape=(jax.ShapeDtypeStruct((n_table, 25...  39.7 us
    pallas_call x1, Pallas kernels, scatter_rows(): pl.pallas_call(scatter_kernel, out_shape=pltpu.VMEM((total_slots, width),...  20.9 us

profile of v6, /device:TPU:2, one launch (start us, length us, event | category | flops | bytes accessed | tf_op | source)
XLA Modules:
  0.0 104.6 jit_solution(17999359571724040509)
XLA Ops:
  0.6 39.7 %shard_map.187 = (bf16[16,256,128]{2,1,0:T(8,128)(2,1)}, bf16[4,144,1024]{2,1,0:T(8,128)(2,1)}) custom-call(bf16[256,128]{1,0:T(8,128)(2,1)} %dense_feat.1, bf16[256,2048]{1,0:T(8,128)(2,1)} %pooled.1, bf16[2176,256]{1,0:T(8,128)(2,1)} %cross_down.1, bf16[256,2176]{1,0:T(8,128)(2,1)} %cross_up.1, bf16[2176,1024]{1,0:T(8,128)(2,1)} %w_hidden1.1, ...), custom_call_target="tpu_custom_call" | custom-call | tf_op jit(solution)/shard_map/pallas_call | solution.py:439
  40.3 0.0 copy-start
  40.3 20.9 %shard_map.188 = bf16[16384,128]{1,0:T(8,128)(2,1)S(1)} custom-call(s32[4,65536]{1,0:T(4,128)} %bitcast.10, bf16[4096,128]{1,0:T(8,128)(2,1)} %bitcast.11), custom_call_target="tpu_custom_call" | custom-call | flops 10000000 | bytes 100000000 | tf_op jit(solution)/shard_map/pallas_call | solution.py:898
  61.3 0.0 copy-done
  61.3 42.1 %shard_map.189 = (f32[1024,128]{1,0:T(8,128)S(1)}, bf16[2,8,144,128]{3,2,1,0:T(8,128)(2,1)S(1)}) custom-call(bf16[16,1024,128]{2,1,0:T(8,128)(2,1)S(1)} %bitcast.9, bf16[4,144,1024]{2,1,0:T(8,128)(2,1)S(1)} %copy-done), custom_call_target="tpu_custom_call" | custom-call | tf_op jit(solution)/shard_map/pallas_call | solution.py:795
  103.4 1.3 %shard_map.190 = (f32[1,1024,128]{2,1,0:T(8,128)}, f32[136,256]{1,0:T(8,128)}, f32[16,2176]{1,0:T(8,128)}, f32[136]{0:T(256)}, f32[136,1024]{1,0:T(8,128)}, /*in...) custom-call(bf16[2,8,144,128]{3,2,1,0:T(8,128)(2,1)S(1)} %get-tuple-element.15.final, ...), custom_call_target="tpu_custom_call" | custom-call | tf_op jit(solution)/shard_map/pallas_call | solution.py:781
Async XLA Ops:
  40.3 20.9 %copy-start = (bf16[4,144,1024]{2,1,0:T(8,128)(2,1)S(1)}, bf16[4,144,1024]{2,1,0:T(8,128)(2,1)}, u32[]{:S(2)}) copy-start(bf16[4,144,1024]{2,1,0:T(8,128)(2,1)} %get-tuple-element.14.dense_mid) | copy-start | bytes 3538948

commit v7 on v6

--- a/solution.py
+++ b/solution.py
@@ -255,7 +255,7 @@
 
     tiles(back_stacked, 2176)
     pl.semaphore_wait(barrier, n_table + 1)
-    for d in range(1, n_table):
+    for d in sorted(range(1, n_table), key=lambda d: (abs(d - Z), d)):
         exchange_table(d).start()
     own_table().start()
 
@@ -549,6 +549,7 @@
     pl.semaphore_wait(barrier, len(peers))
 
     half = rows // 2
+    far_first = (4, 3, 5, 2, 6, 1, 7)
 
     def ring1(j):
         return ring(
@@ -683,14 +684,14 @@
             zparts[k, at, :] = total[:, 128 * k : 128 * k + 128]
 
     blocks(PIECE // 16, 16, dense_last)
-    for d in range(1, Z):
+    for d in far_first:
         copyz(d).start()
     forward(3)
     go(ring1(0), 2, 3)
     for d in range(1, Z):
         copyz(d).wait_recv()
     final[core, z] = add_up(zparts[z], *[zgot[d - 1] for d in range(1, Z)]).astype(bf16)
-    for d in range(1, Z):
+    for d in far_first:
         copyg(d, z).start()
     row_mid(2)
     go(ring2(), 0, 1)

time: 107 us -> 106 us (level); the launches traced: 105 us -> 105 us
    pallas_call x1, Pallas kernels: 39.7 us -> 41 us  [dense_part(): pl.pallas_call(dense_kernel, out_shape=(jax.ShapeDtypeStruct((n_table, 25...]
where the time goes in v7:
time: 106 us; the launch traced here: 105 us
  Pallas kernels  104 us (98%)
    pallas_call x1, Pallas kernels, exchange(): pl.pallas_call(exchange_kernel, out_shape=(jax.ShapeDtypeStruct((rows, wi...  41 us
    pallas_call x1, Pallas kernels, dense_part(): pl.pallas_call(dense_kernel, out_shape=(jax.ShapeDtypeStruct((n_table, 25...  41 us
    pallas_call x1, Pallas kernels, scatter_rows(): pl.pallas_call(scatter_kernel, out_shape=pltpu.VMEM((total_slots, width),...  20.9 us

profile of v7, /device:TPU:2, one launch (start us, length us, event | category | flops | bytes accessed | tf_op | source)
XLA Modules:
  0.0 104.9 jit_solution(15331552819728481411)
XLA Ops:
  0.6 41.0 %shard_map.187 = (bf16[16,256,128]{2,1,0:T(8,128)(2,1)}, bf16[4,144,1024]{2,1,0:T(8,128)(2,1)}) custom-call(bf16[256,128]{1,0:T(8,128)(2,1)} %dense_feat.1, bf16[256,2048]{1,0:T(8,128)(2,1)} %pooled.1, bf16[2176,256]{1,0:T(8,128)(2,1)} %cross_down.1, bf16[256,2176]{1,0:T(8,128)(2,1)} %cross_up.1, bf16[2176,1024]{1,0:T(8,128)(2,1)} %w_hidden1.1, ...), custom_call_target="tpu_custom_call" | custom-call | tf_op jit(solution)/shard_map/pallas_call | solution.py:439
  41.7 0.0 copy-start
  41.7 20.9 %shard_map.188 = bf16[16384,128]{1,0:T(8,128)(2,1)S(1)} custom-call(s32[4,65536]{1,0:T(4,128)} %bitcast.10, bf16[4096,128]{1,0:T(8,128)(2,1)} %bitcast.11), custom_call_target="tpu_custom_call" | custom-call | flops 10000000 | bytes 100000000 | tf_op jit(solution)/shard_map/pallas_call | solution.py:899
  62.6 0.0 copy-done
  62.6 41.0 %shard_map.189 = (f32[1024,128]{1,0:T(8,128)S(1)}, bf16[2,8,144,128]{3,2,1,0:T(8,128)(2,1)S(1)}) custom-call(bf16[16,1024,128]{2,1,0:T(8,128)(2,1)S(1)} %bitcast.9, bf16[4,144,1024]{2,1,0:T(8,128)(2,1)S(1)} %copy-done), custom_call_target="tpu_custom_call" | custom-call | tf_op jit(solution)/shard_map/pallas_call | solution.py:796
  103.7 1.3 %shard_map.190 = (f32[1,1024,128]{2,1,0:T(8,128)}, f32[136,256]{1,0:T(8,128)}, f32[16,2176]{1,0:T(8,128)}, f32[136]{0:T(256)}, f32[136,1024]{1,0:T(8,128)}, /*in...) custom-call(bf16[2,8,144,128]{3,2,1,0:T(8,128)(2,1)S(1)} %get-tuple-element.15.final, ...), custom_call_target="tpu_custom_call" | custom-call | tf_op jit(solution)/shard_map/pallas_call | solution.py:782
Async XLA Ops:
  41.7 20.9 %copy-start = (bf16[4,144,1024]{2,1,0:T(8,128)(2,1)S(1)}, bf16[4,144,1024]{2,1,0:T(8,128)(2,1)}, u32[]{:S(2)}) copy-start(bf16[4,144,1024]{2,1,0:T(8,128)(2,1)} %get-tuple-element.14.dense_mid) | copy-start | bytes 3538948
